TPU v7x, 32 devices: a whole 2x2x4 slice. The times are simulated.
32 devices in a mesh: row: 8 (over y, x, core), col: 4 (over z).
Axes of the slice: x: 2, y: 2, z: 4, core: 2. Of those that a mesh axis runs over, the one named last changes fastest.
Arguments:
- panel: float32 [32768, 256], P(('row', 'col')), may hold values from -8 to 8
- diag_inverse: float32 [256, 256], replicated
- tiles: bfloat16 [8704, 256, 256], P(('row', 'col')), may hold values from -6 to 6
- tile_map: int32 [8704, 2], P(('row', 'col')), may hold values from -1 to 31, as said below
- send_list: int32 [256], P(('row', 'col')), may hold values from -1 to 271, as said below
- place_list: int32 [8448], P(('row', 'col')), may hold values from -1 to 279, as said below
Outputs:
- factor_panel: float32 [32768, 256], P(('row', 'col'))
- balanced: bfloat16 [8448, 256, 256], P(('row', 'col'))
Inputs may be any that keep to these rules, and one draw needn't show every extreme that they name: `tile_map`: each lower tile (I >= J) owned block-cyclically by a device appears in exactly one of its slots, in a drawn order; its other slots hold -1 in both entries. `send_list`: entries of a device name distinct live slots of that device, those it hands to its partner; unused entries are -1 and stand after the used ones. `place_list`: over a device's 264 entries, every live slot it does not hand over and every used send entry of its partner appear exactly once, in a drawn order; the rest are -1.
All inputs are finite; a program needn't handle non-finite values.
Results may differ from a plain program's by a relative error of at most 0.0051.
Values may be sent and summed in bfloat16 or wider, within the bound.
No kernel may reach another device: no remote copies, remote signals or barrier semaphores. Data moves between devices by JAX's collectives and lax.ppermute only.
A program may use at most 256 MiB of HBM per device.

v0:
```python
import jax
import jax.numpy as jnp
from jax import lax
from jax.sharding import PartitionSpec as P


def swapped(value, axis, stride):
    mask = 2**stride
    pairs = [(source, source ^ mask) for source in range(lax.axis_size(axis))]
    return lax.ppermute(value, axis, pairs)


def pick_tiles(stack_tiles, index_list):
    return jnp.take(stack_tiles, index_list, axis=0)


def renew_tiles(raw_block, left_block, right_block):
    product = jnp.einsum(
        "sik,sjk->sij", left_block, right_block, preferred_element_type=jnp.float32
    )
    return (raw_block.astype(jnp.float32) - product).astype(jnp.bfloat16)


def shards(panel, diag_inverse, tiles, tile_map, send_list, place_list):
    slot_count = tiles.shape[0]
    tile_size = tiles.shape[1]
    move_count = send_list.shape[0]
    row_count = lax.axis_size("row")
    col_count = lax.axis_size("col")
    column = lax.axis_index("col")
    groups = row_count // col_count
    bit_count = row_count.bit_length() - 1
    zero_half = jnp.zeros((), jnp.bfloat16)
    send_valid = send_list >= 0
    send_safe = jnp.clip(send_list, 0, slot_count - 1)
    factor = jnp.dot(
        panel, diag_inverse.T, precision=lax.Precision.HIGHEST, preferred_element_type=jnp.float32
    )
    row_block = lax.all_gather(factor.astype(jnp.bfloat16), "col", axis=0, tiled=True)
    row_tiles = row_block.reshape(-1, tile_size, tile_size)
    row_local = row_tiles.shape[0]
    everything = lax.all_gather(row_tiles, "row", axis=0, tiled=True)
    shaped = everything.reshape(groups, col_count, row_local, tile_size, tile_size)
    picked = lax.dynamic_index_in_dim(shaped, column, 1, keepdims=False)
    col_tiles = picked.reshape(-1, tile_size, tile_size)
    row_pick = jnp.clip(tile_map[:, 0], 0, row_local - 1)
    col_pick = jnp.clip(tile_map[:, 1], 0, groups * row_local - 1)
    col_flat = col_pick % groups * row_local + col_pick // groups
    left_all = pick_tiles(row_tiles, row_pick)
    right_all = pick_tiles(col_tiles, col_flat)
    renewed_all = renew_tiles(tiles, left_all, right_all)
    outgoing_new = jnp.where(
        send_valid[:, None, None], pick_tiles(renewed_all, send_safe), zero_half
    )
    for bit_index in range(bit_count):
        outgoing_new = swapped(outgoing_new, "row", bit_index)
    tile_pool = jnp.concatenate([renewed_all, outgoing_new], 0)
    renewed = pick_tiles(tile_pool, jnp.clip(place_list, 0, slot_count + move_count - 1))
    balanced = jnp.where((place_list >= 0)[:, None, None], renewed, zero_half)
    return (factor, balanced)


def solution(mesh):
    in_specs = (
        P(("row", "col"), None),
        P(),
        P(("row", "col"), None, None),
        P(("row", "col"), None),
        P(("row", "col")),
        P(("row", "col")),
    )
    out_specs = (P(("row", "col"), None), P(("row", "col"), None, None))
    return jax.shard_map(shards, mesh=mesh, in_specs=in_specs, out_specs=out_specs, check_vma=False)
```

profile of v0, /device:TPU:0, one launch (start us, length us, event | category | flops | bytes accessed | tf_op | source)
XLA Modules:
  0.0 355.3 jit_solution(4321126421967017418)
XLA Ops:
  7.2 0.0 copy-start
  7.2 0.0 all-gather.3.cloned.1.call-start
  7.2 1.2 copy-done
  8.4 3.1 fusion.13
  11.5 0.0 all-gather.3.cloned.1.call-update
  11.5 0.0 all-gather.5.cloned.1.call-start
  11.6 48.7 %all-gather.3.cloned.1.call-done = bf16[4096,256]{1,0:T(8,128)(2,1)} async-done(((bf16[1024,256]{1,0:T(8,128)(2,1)}), bf16[4096,256]{1,0:T(8,128)(2,1)}) %all-gather.3.cloned.1.call-update) | async-done | bytes 2097168 | tf_op jit(solution)/shard_map/all_gather | solution.py:39
  60.3 0.0 all-gather.5.cloned.1.call-update
  60.4 0.8 and_reduce_fusion.1
  61.2 0.7 compare_and_fusion
  61.9 17.5 %gather_fusion = bf16[272,256,256]{2,1,0:T(8,128)(2,1)} fusion(bf16[16,256,256]{2,1,0:T(8,128)(2,1)} %bitcast.6, s32[1024]{0:T(1024)S(1)} %pad_clamp_fusion.3), kind=kCustom, calls=%fused_computation | custom fusion | bytes 71304256 | tf_op jit(solution)/shard_map/jit(_take)/gather | solution.py:14
  79.4 71.4 %all-gather.5.cloned.1.call-done = bf16[128,256,256]{2,1,0:T(8,128)(2,1)} async-done(((bf16[16,256,256]{2,1,0:T(8,128)(2,1)}), bf16[128,256,256]{2,1,0:T(8,128)(2,1)}) %all-gather.5.cloned.1.call-update) | async-done | bytes 16777232 | tf_op jit(solution)/shard_map/all_gather | solution.py:42
  150.8 4.6 %constant_dynamic-slice_fusion = bf16[2,1,16,256,256]{4,3,2,1,0:T(8,128)(2,1)} fusion(bf16[2,4,16,256,256]{4,3,2,1,0:T(8,128)(2,1)} %bitcast.8, s32[]{:T(128)S(6)} %select_n.72), kind=kLoop, calls=%fused_computation.35 | loop fusion | bytes 8388612 | tf_op jit(solution)/shard_map/jit(dynamic_index_in_dim)/dynamic_slice | solution.py:44
  155.5 17.1 %gather_fusion.1 = bf16[272,256,256]{2,1,0:T(8,128)(2,1)} fusion(bf16[32,256,256]{2,1,0:T(8,128)(2,1)} %bitcast.7, s32[1024]{0:T(1024)S(1)} %pad_clamp_fusion.2), kind=kCustom, calls=%fused_computation.1 | custom fusion | bytes 71304256 | tf_op jit(solution)/shard_map/jit(_take)/gather | solution.py:14
  172.5 0.0 copy-start.2
  172.5 46.7 %subtract_convert_fusion = bf16[272,256,256]{2,1,0:T(8,128)(2,1)} fusion(bf16[272,256,256]{2,1,0:T(8,128)(2,1)} %param.8, bf16[272,256,256]{2,1,0:T(8,128)(2,1)} %gather_fusion.1, pred[272]{0:T(512)(128)(4,1)S(1)} %get-tuple-element.8, bf16[272,256,256]{2,1,0:T(8,128)(2,1)} %gather_fusion, pred[272]{0:T(512)(128)(4,1)S(1)} %get-tuple-element.4), kind=kOutput, calls=%fused_computation.4 | convolution fusion | flops 9215934464 | bytes 142606880 | tf_op jit(solution)/shard_map/sik,sjk->sij/dot_general | solution.py:18
  219.2 2.3 gather_fusion.2
  221.6 0.2 select_select_fusion.1
  221.8 0.3 collective-permute-start
  222.1 2.4 collective-permute-done
  224.5 1.4 collective-permute-start.1
  225.9 23.9 %collective-permute-done.1 = bf16[8,256,256]{2,1,0:T(8,128)(2,1)S(1)} collective-permute-done((bf16[8,256,256]{2,1,0:T(8,128)(2,1)S(1)}, bf16[8,256,256]{2,1,0:T(8,128)(2,1)S(1)}, u32[]{:S(2)}, u32[]{:S(2)}) %collective-permute-start.1) | collective-permute-done | bytes 1048608 | tf_op jit(solution)/shard_map/ppermute | solution.py:10
  249.8 0.3 collective-permute-start.2
  250.1 0.0 copy-done.2
  250.1 24.2 %collective-permute-done.2 = bf16[8,256,256]{2,1,0:T(8,128)(2,1)S(1)} collective-permute-done((bf16[8,256,256]{2,1,0:T(8,128)(2,1)S(1)}, bf16[8,256,256]{2,1,0:T(8,128)(2,1)S(1)}, u32[]{:S(2)}, u32[]{:S(2)}) %collective-permute-start.2) | collective-permute-done | bytes 1048608 | tf_op jit(solution)/shard_map/ppermute | solution.py:10
  274.4 24.5 %pad_maximum_fusion = bf16[280,256,256]{2,1,0:T(8,128)(2,1)} fusion(bf16[8,256,256]{2,1,0:T(8,128)(2,1)S(1)} %collective-permute-done.2, bf16[272,256,256]{2,1,0:T(8,128)(2,1)} %subtract_convert_fusion), kind=kLoop, calls=%fused_computation.5 | loop fusion | flops 18350080 | bytes 73400320 | tf_op jit(solution)/shard_map/concatenate | solution.py:57
  298.9 0.0 copy-start.1
  298.9 26.0 %gather_fusion.3 = bf16[264,256,256]{2,1,0:T(8,128)(2,1)} fusion(bf16[280,256,256]{2,1,0:T(8,128)(2,1)} %pad_maximum_fusion, s32[1024]{0:T(1024)S(1)} %pad_clamp_fusion), kind=kCustom, calls=%fused_computation.3 | custom fusion | bytes 69207072 | tf_op jit(solution)/shard_map/jit(_take)/gather | solution.py:14
  324.9 23.5 %select_select_fusion = bf16[264,256,256]{2,1,0:T(8,128)(2,1)} fusion(bf16[264,256,256]{2,1,0:T(8,128)(2,1)} %gather_fusion.3, pred[264]{0:T(512)(128)(4,1)S(1)} %get-tuple-element.11, pred[264]{0:T(512)(128)(4,1)S(1)} %get-tuple-element.10), kind=kLoop, calls=%fused_computation.11 | loop fusion | flops 34603008 | bytes 69206544 | tf_op jit(solution)/shard_map/jit(_where)/select_n | solution.py:59
  348.4 0.0 copy-done.1
  (8 shorter events, 0.1 us)
Async XLA Ops:
  7.2 1.2 copy-start
  7.2 53.1 %all-gather.3.cloned.1.call-start = ((), (), s32[]{:S(2)}) async-start(), calls=%async_computation | async-start | bytes 2621440 | tf_op jit(solution)/shard_map/all_gather | solution.py:39
  11.5 139.3 %all-gather.5.cloned.1.call-start = ((), (), s32[]{:S(2)}) async-start(), calls=%async_computation.1 | async-start | bytes 18874368 | tf_op jit(solution)/shard_map/all_gather | solution.py:42
  172.5 77.6 %copy-start.2 = (s32[264]{0:T(512)S(1)}, s32[264]{0:T(512)}, u32[]{:S(2)}) copy-start(s32[264]{0:T(512)} %param.11) | copy-start | bytes 3172
  221.8 2.7 collective-permute-start
  224.5 25.3 %collective-permute-start.1 = (bf16[8,256,256]{2,1,0:T(8,128)(2,1)S(1)}, bf16[8,256,256]{2,1,0:T(8,128)(2,1)S(1)}, u32[]{:S(2)}, u32[]{:S(2)}) collective-permute-start(bf16[8,256,256]{2,1,0:T(8,128)(2,1)S(1)} %collective-permute-done), channel_id=1, source_target_pairs={{0,8},{4,12},{8,0},{12,4},{16,24},{20,28},{24,16},{28,20},{1,9},{5... | collective-permute-start | bytes 3145736 | tf_op jit(solution)/shard_map/ppermute | solution.py:10
  249.8 24.5 %collective-permute-start.2 = (bf16[8,256,256]{2,1,0:T(8,128)(2,1)S(1)}, bf16[8,256,256]{2,1,0:T(8,128)(2,1)S(1)}, u32[]{:S(2)}, u32[]{:S(2)}) collective-permute-start(bf16[8,256,256]{2,1,0:T(8,128)(2,1)S(1)} %collective-permute-done.1), channel_id=1, source_target_pairs={{0,16},{4,20},{8,24},{12,28},{16,0},{20,4},{24,8},{28,12},{1,17},{... | collective-permute-start | bytes 3145736 | tf_op jit(solution)/shard_map/ppermute | solution.py:10
  298.9 49.5 %copy-start.1 = (f32[1024,256]{1,0:T(8,128)S(1)}, f32[1024,256]{1,0:T(8,128)}, u32[]{:S(2)}) copy-start(f32[1024,256]{1,0:T(8,128)} %param.6) | copy-start | bytes 3145732
Sparse Core Ops, SparseCore 0:
  11.6 48.6 all-gather.2
  62.2 88.5 all-gather.4
where the time goes:
time: 356 us; the launch traced here: 355 us
  waiting for transfers between devices  171 us (48%)
  local copies, waits for them, and re-layouts  68.8 us (19%)
  matrix products  49.8 us (14%)
  other arithmetic  49.7 us (14%)
  between operations  14.1 us (4%)
    all_gather x1, waiting for transfers between devices, shards(): everything = lax.all_gather(row_tiles, 'row', axis=0, tiled=True)  71.4 us
    gather x4, local copies, waits for them, and re-layouts, pick_tiles(): return jnp.take(stack_tiles, index_list, axis=0)  63 us
    ppermute x3, waiting for transfers between devices, swapped(): return lax.ppermute(value, axis, pairs)  50.5 us
    all_gather x1, waiting for transfers between devices, shards(): lax.all_gather(factor.astype(jnp.bfloat16), 'col', axis=0, tiled=True)  48.7 us
    dot_general x1, matrix products, renew_tiles(): jnp.einsum('sik,sjk->sij', left_block, right_block, preferred_element_typ...  46.7 us
    concatenate x1, other arithmetic, shards(): tile_pool = jnp.concatenate([renewed_all, outgoing_new], 0)  24.5 us
    select_n x1, other arithmetic, shards(): balanced = jnp.where((place_list >= 0)[:, None, None], renewed, zero_half)  23.5 us
  transfers between devices with their start and end apart: 5, of which 5 were waited for; matrix products, arithmetic and copies ran while one was open for 5% of the time, Pallas kernels for 0%

commit v1 on v0

v1 whole, which is shorter than its diff:
```python
import functools
import jax
import jax.numpy as jnp
from jax import lax
from jax.experimental import pallas as pl
from jax.experimental.pallas import tpu as pltpu
from jax.sharding import PartitionSpec as P

AXES = ("row", "col")
RING = 6
VMEM_LIMIT = 24 * 1024 * 1024


def tied(value, *others):
    return lax.optimization_barrier((value,) + others)[0]


def across(value, row, column, row_count, col_count):
    known = col_count - 1
    for bit in range(col_count.bit_length() - 2, 0, -1):
        received = lax.ppermute(value, AXES, spread_pairs(bit, known, row_count, col_count))
        known &= ~(1 << bit)
        value = jnp.where(((row ^ column) >> bit) & 1 == 0, value, received)
    return value


def exchanged(value, known, row_count, col_count):
    pieces = [value]
    for bit in range(col_count.bit_length() - 1, row_count.bit_length() - 1):
        pieces = pieces + [
            lax.ppermute(piece, AXES, spread_pairs(bit, known, row_count, col_count)) for piece in pieces
        ]
    return pieces


def spread_pairs(bit, known, row_count, col_count):
    chosen = []
    for source in range(row_count):
        for place in range(col_count):
            if (source ^ place) & known == 0:
                chosen.append((source * col_count + place, (source ^ (1 << bit)) * col_count + place))
    return chosen


def gather_and_spread(half, early, row, column, row_count, col_count):
    sizes = (row_count, col_count)

    def forward(part):
        value = across(part, row, column, *sizes)
        return exchanged(value, 1, *sizes)

    def to_other_core(near):
        return lax.ppermute(near, AXES, spread_pairs(0, 1, *sizes))

    def z_pairs(hops, wanted):
        return [
            (place * col_count + source, place * col_count + target)
            for place in range(row_count)
            for source, target in hops
            if (place % col_count == target) == wanted
        ]

    parts = [half]
    for mask in range(1, min(col_count, 3)):
        parts.append(lax.ppermute(half, "col", [(place, place ^ mask) for place in range(col_count)]))
    pieces = [forward(tied(half, early))]
    if col_count == 4:
        outer, inner = [(1, 0), (2, 3)], [(1, 2), (2, 1)]
        at_end = (column == 0) | (column == 3)
        near = [jnp.concatenate(pieces[0], 0)]
        middle = lax.ppermute(tied(half, parts[2]), AXES, z_pairs(inner, True))
        onward = lax.ppermute(tied(parts[2], pieces[0][-1], parts[1]), AXES, z_pairs(outer, True))
        first = jnp.where(at_end, onward, middle)
        turned = jnp.concatenate(exchanged(parts[2], col_count - 1, *sizes), 0)
        pieces.append(forward(parts[1]))
        middle = lax.ppermute(tied(half, parts[1], parts[2]), AXES, z_pairs(inner, False))
        onward = lax.ppermute(tied(parts[2], parts[1]), AXES, z_pairs(outer, False))
        near.append(jnp.concatenate(pieces[1], 0))
        near.append(across(tied(turned, first), row, column, *sizes))
        near.append(jnp.concatenate(forward(first), 0))
        parts += [first, onward, middle]
        near[1] = tied(near[1], onward, middle)
        near[3] = tied(near[3], near[2])
        far = [to_other_core(held) for held in near]
    else:
        for mask in range(len(parts), col_count):
            parts.append(lax.ppermute(half, "col", [(place, place ^ mask) for place in range(col_count)]))
        pieces += [forward(part) for part in parts[1:]]
        near = [jnp.concatenate(held, 0) for held in pieces]
        far = [to_other_core(held) for held in near]
    return parts, near, far


def renew_kernel(sizes, source_list, cell_list, *refs):
    col_count, groups, row_local, part_rows, slot_count, count, batch, ring = sizes
    part_count = len(refs) - 2 * col_count - 10
    row_parts, refs = refs[:part_count], refs[part_count:]
    col_near, refs = refs[:col_count], refs[col_count:]
    col_far, refs = refs[:col_count], refs[col_count:]
    tiles, out, row_buf, col_buf, in_buf, out_buf, row_sem, col_sem, in_sem, out_sem = refs
    tile_size = tiles.shape[1]
    steps = count // batch
    row = lax.axis_index("row")
    column = lax.axis_index("col")

    def fetch(step, slot):
        for t in range(batch):
            chosen = jnp.clip(source_list[step * batch + t], 0, slot_count - 1)
            pltpu.make_async_copy(tiles.at[chosen], in_buf.at[slot, t], in_sem.at[slot]).start()

    def cell(index):
        chosen = jnp.clip(source_list[index], 0, slot_count - 1)
        at_col = jnp.maximum(cell_list[1, chosen], 0)
        return jnp.maximum(cell_list[0, chosen], 0), lax.rem(at_col, groups), at_col // groups

    def stage(source, target, at, sem):
        pltpu.make_async_copy(source, target.at[pl.ds(pl.multiple_of(at, part_rows), part_rows)], sem).start()

    leads = lax.rem(row, col_count) == column
    at_end = (column == 0) | (column == col_count - 1)
    cases = (leads, jnp.logical_not(leads) & at_end, jnp.logical_not(leads | at_end))
    row_entries = [(entry, mask, None) for mask, entry in enumerate(row_parts[:col_count])]
    if part_count > col_count:
        last = col_count - 1
        row_entries = row_entries[:last] + [(entry, last, case) for entry, case in zip(row_parts[last:], cases)]
    is_near = (row ^ column) & 1 == 0

    def stage_all():
        for entry, mask, case in row_entries:
            @pl.when(True if case is None else case)
            def _(entry=entry, mask=mask):
                stage(entry, row_buf, (column ^ mask) * part_rows, row_sem)

        for held, wanted in ((col_near, is_near), (col_far, jnp.logical_not(is_near))):
            @pl.when(wanted)
            def _(held=held):
                for mask in range(col_count):
                    for piece in range(groups):
                        group = (row // col_count) ^ piece
                        at = (group * col_count + (column ^ mask)) * part_rows
                        stage(held[mask].at[pl.ds(piece * part_rows, part_rows)], col_buf, at, col_sem)

    early = min(2, ring, steps)
    for step in range(early):
        fetch(step, step)
    stage_all()
    for step in range(early, min(ring, steps)):
        fetch(step, step)
    pltpu.make_async_copy(row_buf, row_buf, row_sem).wait()
    pltpu.make_async_copy(col_buf, col_buf, col_sem).wait()

    def body(step, carry):
        slot = lax.rem(step, ring)
        pltpu.make_async_copy(in_buf.at[slot], in_buf.at[slot], in_sem.at[slot]).wait()

        @pl.when(step >= ring)
        def _():
            pltpu.make_async_copy(out_buf.at[slot], out_buf.at[slot], out_sem.at[slot]).wait()

        for t in range(batch):
            source = source_list[step * batch + t]
            at_row, group, at_col = cell(step * batch + t)
            at_flat = group * row_local + at_col
            left = row_buf[pl.ds(pl.multiple_of(at_row * tile_size, tile_size), tile_size), :]
            right = col_buf[pl.ds(pl.multiple_of(at_flat * tile_size, tile_size), tile_size), :]
            product = lax.dot_general(left, right, (((1,), (1,)), ((), ())), preferred_element_type=jnp.float32)
            fresh = in_buf[slot, t].astype(jnp.float32) - product
            out_buf[slot, t] = jnp.where(source >= 0, fresh, 0.0).astype(jnp.bfloat16)
        pltpu.make_async_copy(out_buf.at[slot], out.at[pl.ds(step * batch, batch)], out_sem.at[slot]).start()

        @pl.when(step + ring < steps)
        def _():
            fetch(step + ring, slot)

        return carry

    lax.fori_loop(0, steps, body, 0)
    for step in range(max(0, steps - ring), steps):
        slot = step % ring
        pltpu.make_async_copy(out_buf.at[slot], out_buf.at[slot], out_sem.at[slot]).wait()


def renew(source_list, cell_list, row_parts, col_near, col_far, tiles, groups, batch_most):
    slot_count, tile_size, _ = tiles.shape
    count = source_list.shape[0]
    part_rows = row_parts[0].shape[0]
    col_count = len(col_near)
    row_local = col_count * part_rows // tile_size
    batch = max(size for size in range(1, batch_most + 1) if count % size == 0)
    ring = min(RING, count // batch)
    sizes = (col_count, groups, row_local, part_rows, slot_count, count, batch, ring)
    operands = list(row_parts) + list(col_near) + list(col_far) + [tiles]
    tile_bytes = tile_size * tile_size * 2
    return pl.pallas_call(
        functools.partial(renew_kernel, sizes),
        out_shape=jax.ShapeDtypeStruct((count, tile_size, tile_size), jnp.bfloat16),
        grid_spec=pltpu.PrefetchScalarGridSpec(
            num_scalar_prefetch=2,
            grid=(),
            in_specs=[pl.BlockSpec(memory_space=pl.ANY)] * len(operands),
            out_specs=pl.BlockSpec(memory_space=pl.ANY),
            scratch_shapes=[
                pltpu.VMEM((row_local * tile_size, tile_size), jnp.bfloat16),
                pltpu.VMEM((groups * row_local * tile_size, tile_size), jnp.bfloat16),
                pltpu.VMEM((ring, batch, tile_size, tile_size), jnp.bfloat16),
                pltpu.VMEM((ring, batch, tile_size, tile_size), jnp.bfloat16),
                pltpu.SemaphoreType.DMA,
                pltpu.SemaphoreType.DMA,
                pltpu.SemaphoreType.DMA((ring,)),
                pltpu.SemaphoreType.DMA((ring,)),
            ],
        ),
        compiler_params=pltpu.CompilerParams(vmem_limit_bytes=VMEM_LIMIT),
        cost_estimate=pl.CostEstimate(
            flops=2 * count * tile_size**3,
            bytes_accessed=2 * count * tile_bytes + (1 + groups) * row_local * tile_bytes,
            transcendentals=0,
        ),
    )(source_list, cell_list, *operands)


def place_kernel(places, incoming, held, out, sem):
    del held
    count = incoming.shape[0]
    for index in range(count):
        @pl.when(places[index] >= 0)
        def _():
            pltpu.make_async_copy(incoming.at[index], out.at[places[index]], sem.at[index]).start()
    for index in range(count):
        @pl.when(places[index] >= 0)
        def _():
            pltpu.make_async_copy(incoming.at[index], out.at[places[index]], sem.at[index]).wait()


def place(places, incoming, held):
    return pl.pallas_call(
        place_kernel,
        out_shape=jax.ShapeDtypeStruct(held.shape, held.dtype),
        grid_spec=pltpu.PrefetchScalarGridSpec(
            num_scalar_prefetch=1,
            grid=(),
            in_specs=[pl.BlockSpec(memory_space=pltpu.VMEM), pl.BlockSpec(memory_space=pl.ANY)],
            out_specs=pl.BlockSpec(memory_space=pl.ANY),
            scratch_shapes=[pltpu.SemaphoreType.DMA((incoming.shape[0],))],
        ),
        input_output_aliases={2: 0},
        compiler_params=pltpu.CompilerParams(vmem_limit_bytes=4 * 1024 * 1024),
    )(places, incoming, held)


def shards(panel, diag_inverse, tiles, tile_map, send_list, place_list):
    slot_count = tiles.shape[0]
    move_count = send_list.shape[0]
    row_count = lax.axis_size("row")
    col_count = lax.axis_size("col")
    row = lax.axis_index("row")
    column = lax.axis_index("col")
    groups = row_count // col_count
    factor = jnp.dot(
        panel, diag_inverse.T, precision=lax.Precision.HIGH, preferred_element_type=jnp.float32
    )
    half = factor.astype(jnp.bfloat16)

    wanted = slot_count + jnp.arange(move_count, dtype=jnp.int32)
    spots = jnp.arange(place_list.shape[0], dtype=jnp.int32)
    places = jnp.max(jnp.where(place_list[None, :] == wanted[:, None], spots[None, :], -1), axis=1)

    row_parts, near, far = gather_and_spread(half, places, row, column, row_count, col_count)

    renewing = functools.partial(
        renew, cell_list=tile_map.T, row_parts=row_parts, col_near=near, col_far=far,
        tiles=tiles, groups=groups,
    )
    outgoing = renewing(send_list, batch_most=2)
    incoming = lax.ppermute(outgoing, "row", [(source, row_count - 1 - source) for source in range(row_count)])
    held = renewing(place_list, batch_most=8)
    balanced = place(places, incoming, held)
    return (factor, balanced)


def solution(mesh):
    in_specs = (
        P(("row", "col"), None),
        P(),
        P(("row", "col"), None, None),
        P(("row", "col"), None),
        P(("row", "col")),
        P(("row", "col")),
    )
    out_specs = (P(("row", "col"), None), P(("row", "col"), None, None))
    return jax.shard_map(shards, mesh=mesh, in_specs=in_specs, out_specs=out_specs, check_vma=False)
```

time: 356 us -> 104 us (0.29)
  waiting for transfers between devices: 171 us -> 34.1 us
  local copies, waits for them, and re-layouts: 68.8 us -> 1.09 us
  matrix products: 49.8 us -> 2.54 us
  other arithmetic: 49.7 us -> 2.67 us
  starting transfers between devices: 2.14 us -> 32.6 us
  Pallas kernels: 0 us -> 28.9 us
  between operations: 14.1 us -> 0.98 us
    all_gather x2 -> x0, waiting for transfers between devices: 120 us -> none  [the longest x1 71.4 us: shards(): everything = lax.all_gather(row_tiles, 'row', axis=0, tiled=True)]
    gather x4 -> x0, local copies, waits for them, and re-layouts: 63 us -> none  [pick_tiles(): return jnp.take(stack_tiles, index_list, axis=0)]
    dot_general x2 -> x1, matrix products: 49.8 us -> 2.54 us  [shards(): jnp.dot(panel, diag_inverse.T, precision=lax.Precision.HIGH, preferred_el...]
    ppermute x3 -> x19, starting transfers between devices: 2.06 us -> 32.6 us  [the longest x4 12.9 us: exchanged(): lax.ppermute(piece, AXES, spread_pairs(bit, known, row_count, col_count))]
    pallas_call x0 -> x3, Pallas kernels: none -> 28.9 us  [the longest x2 27.3 us: renew(): pl.pallas_call(functools.partial(renew_kernel, sizes), out_shape=jax.Shap...]
    select_n x5, other arithmetic: 23.7 us -> 0.4 us  [the longest x4 0.34 us: across(): value = jnp.where((row ^ column) >> bit & 1 == 0, value, received)]
    concatenate x1 -> x4, other arithmetic: 24.5 us -> 1.32 us  [the longest x1 1.11 us: gather_and_spread(): turned = jnp.concatenate(exchanged(parts[2], col_count - 1, *sizes), 0)]
    ppermute x3 -> x19, waiting for transfers between devices: 50.5 us -> 34.1 us  [the longest x2 12.9 us: gather_and_spread(): lax.ppermute(half, 'col', [(place, place ^ mask) for place in range(col_c...]
  transfers between devices with their start and end apart: 5 -> 19, of which waited for: 5 -> 8; matrix products, arithmetic and copies ran while one was open for 5% -> 2% of each run, Pallas kernels for 0% -> 24%
where the time goes in v1:
time: 104 us; the launch traced here: 103 us
  waiting for transfers between devices  34.1 us (33%)
  starting transfers between devices  32.6 us (31%)
  Pallas kernels  28.9 us (28%)
  other arithmetic  2.67 us (3%)
  matrix products  2.54 us (2%)
  local copies, waits for them, and re-layouts  1.09 us (1%)
    pallas_call x2, Pallas kernels, renew(): pl.pallas_call(functools.partial(renew_kernel, sizes), out_shape=jax.Shap...  27.3 us
    ppermute x2, waiting for transfers between devices, gather_and_spread(): lax.ppermute(half, 'col', [(place, place ^ mask) for place in range(col_c...  12.9 us
    ppermute x4, starting transfers between devices, exchanged(): lax.ppermute(piece, AXES, spread_pairs(bit, known, row_count, col_count))  12.9 us
    ppermute x4, starting transfers between devices, across(): lax.ppermute(value, AXES, spread_pairs(bit, known, row_count, col_count))  9 us
    ppermute x4, waiting for transfers between devices, exchanged(): lax.ppermute(piece, AXES, spread_pairs(bit, known, row_count, col_count))  7.72 us
    ppermute x4, starting transfers between devices, to_other_core(): return lax.ppermute(near, AXES, spread_pairs(0, 1, *sizes))  5.41 us
    ppermute x4, waiting for transfers between devices, across(): lax.ppermute(value, AXES, spread_pairs(bit, known, row_count, col_count))  5.16 us
    ppermute x1, waiting for transfers between devices, gather_and_spread(): lax.ppermute(tied(parts[2], pieces[0][-1], parts[1]), AXES, z_pairs(outer...  4.94 us
  transfers between devices with their start and end apart: 19, of which 8 were waited for; matrix products, arithmetic and copies ran while one was open for 2% of the time, Pallas kernels for 24%

profile of v1, /device:TPU:0, one launch (start us, length us, event | category | flops | bytes accessed | tf_op | source)
XLA Modules:
  0.0 102.9 jit_solution(15389620784387697259)
XLA Ops:
  0.6 0.0 copy-start
  0.7 1.0 select_reduce_fusion.places
  1.6 0.3 copy-done
  1.9 2.5 %fusion = (bf16[1024,256]{1,0:T(8,128)(2,1)S(1)}, f32[1024,256]{1,0:T(8,128)}) fusion(f32[1024,256]{1,0:T(8,128)S(1)} %copy-done, f32[256,256]{1,0:T(8,128)} %param.7), kind=kOutput, calls=%fused_computation.11 | convolution fusion | flops 402915328 | bytes 2883584 | tf_op jit(solution)/shard_map/dot_general | solution.py:259
  4.4 4.9 %collective-permute-start.2 = (bf16[1024,256]{1,0:T(8,128)(2,1)S(1)}, bf16[1024,256]{1,0:T(8,128)(2,1)S(1)}, u32[]{:S(2)}, u32[]{:S(2)}) collective-permute-start(bf16[1024,256]{1,0:T(8,128)(2,1)S(1)} %get-tuple-element.14.refs_0_), channel_id=1, source_target_pairs={{0,8},{5,13},{10,2},{15,7},{16,24},{21,29},{26,18},{31,23}} | collective-permute-start | bytes 1572872 | tf_op jit(solution)/shard_map/ppermute | solution.py:21
  9.3 0.5 collective-permute-start.1
  9.8 1.0 collective-permute-start
  10.8 5.2 %collective-permute-done.2 = bf16[1024,256]{1,0:T(8,128)(2,1)S(1)} collective-permute-done((bf16[1024,256]{1,0:T(8,128)(2,1)S(1)}, bf16[1024,256]{1,0:T(8,128)(2,1)S(1)}, u32[]{:S(2)}, u32[]{:S(2)}) %collective-permute-start.2) | collective-permute-done | bytes 524320 | tf_op jit(solution)/shard_map/ppermute | solution.py:21
  15.9 0.1 broadcast_select_fusion.3
  16.0 3.4 %collective-permute-start.3 = (bf16[1024,256]{1,0:T(8,128)(2,1)S(1)}, bf16[1024,256]{1,0:T(8,128)(2,1)S(1)}, u32[]{:S(2)}, u32[]{:S(2)}) collective-permute-start(bf16[1024,256]{1,0:T(8,128)(2,1)S(1)} %broadcast_select_fusion.3), channel_id=1, source_target_pairs={{0,16},{2,18},{5,21},{7,23},{8,24},{10,26},{13,29},{15,31},{16,0},... | collective-permute-start | bytes 1572872 | tf_op jit(solution)/shard_map/ppermute | solution.py:31
  19.5 12.9 %collective-permute-done.1.refs_2_ = bf16[1024,256]{1,0:T(8,128)(2,1)S(1)} collective-permute-done((bf16[1024,256]{1,0:T(8,128)(2,1)S(1)}, bf16[1024,256]{1,0:T(8,128)(2,1)S(1)}, u32[]{:S(2)}, u32[]{:S(2)}) %collective-permute-start.1) | collective-permute-done | bytes 524320 | tf_op jit(solution)/shard_map/ppermute | solution.py:65
  32.4 0.7 collective-permute-start.5
  33.1 0.0 copy-start.5
  33.1 0.8 copy-done.5
  33.9 1.3 %collective-permute-start.4 = (bf16[1024,256]{1,0:T(8,128)(2,1)S(1)}, bf16[1024,256]{1,0:T(8,128)(2,1)S(1)}, u32[]{:S(2)}, u32[]{:S(2)}) collective-permute-start(bf16[1024,256]{1,0:T(8,128)(2,1)S(1)} %collective-permute-done.1.refs_2_), channel_id=1, source_target_pairs={{1,0},{14,15},{17,16},{30,31}} | collective-permute-start | bytes 1572872 | tf_op jit(solution)/shard_map/ppermute | solution.py:72
  35.2 3.5 %collective-permute-start.10 = (bf16[1024,256]{1,0:T(8,128)(2,1)S(1)}, bf16[1024,256]{1,0:T(8,128)(2,1)}, u32[]{:S(2)}, u32[]{:S(2)}) collective-permute-start(bf16[1024,256]{1,0:T(8,128)(2,1)S(1)} %collective-permute-done.1.refs_2_), channel_id=1, source_target_pairs={{0,16},{5,21},{10,26},{15,31},{16,0},{21,5},{26,10},{31,15}} | collective-permute-start | bytes 1572872 | tf_op jit(solution)/shard_map/ppermute | solution.py:31
  38.7 1.3 %collective-permute-start.8 = (bf16[1024,256]{1,0:T(8,128)(2,1)S(1)}, bf16[1024,256]{1,0:T(8,128)(2,1)S(1)}, u32[]{:S(2)}, u32[]{:S(2)}) collective-permute-start(bf16[1024,256]{1,0:T(8,128)(2,1)S(1)} %collective-permute-done.refs_1_), channel_id=1, source_target_pairs={{0,8},{5,13},{10,2},{15,7},{16,24},{21,29},{26,18},{31,23}} | collective-permute-start | bytes 1572872 | tf_op jit(solution)/shard_map/ppermute | solution.py:21
  40.0 4.9 %collective-permute-done.4 = bf16[1024,256]{1,0:T(8,128)(2,1)S(1)} collective-permute-done((bf16[1024,256]{1,0:T(8,128)(2,1)S(1)}, bf16[1024,256]{1,0:T(8,128)(2,1)S(1)}, u32[]{:S(2)}, u32[]{:S(2)}) %collective-permute-start.4) | collective-permute-done | bytes 524320 | tf_op jit(solution)/shard_map/ppermute | solution.py:72
  44.9 0.1 broadcast_select_fusion.4.refs_3_
  45.0 1.3 %collective-permute-start.12 = (bf16[1024,256]{1,0:T(8,128)(2,1)S(1)}, bf16[1024,256]{1,0:T(8,128)(2,1)S(1)}, u32[]{:S(2)}, u32[]{:S(2)}) collective-permute-start(bf16[1024,256]{1,0:T(8,128)(2,1)S(1)} %broadcast_select_fusion.4.refs_3_), channel_id=1, source_target_pairs={{0,8},{5,13},{10,2},{15,7},{16,24},{21,29},{26,18},{31,23}} | collective-permute-start | bytes 1572872 | tf_op jit(solution)/shard_map/ppermute | solution.py:21
  46.3 0.7 collective-permute-start.6
  47.0 0.7 collective-permute-start.7
  47.7 1.1 %pad_maximum_fusion.2 = bf16[2048,256]{1,0:T(8,128)(2,1)S(1)} fusion(bf16[1024,256]{1,0:T(8,128)(2,1)} %collective-permute-done.10, bf16[1024,256]{1,0:T(8,128)(2,1)S(1)} %collective-permute-done.1.refs_2_), kind=kLoop, calls=%fused_computation.2 | loop fusion | flops 2097152 | bytes 2097152 | tf_op jit(solution)/shard_map/concatenate | solution.py:74
  48.9 0.0 copy-start.6
  48.9 1.5 %collective-permute-start.11 = (bf16[2048,256]{1,0:T(8,128)(2,1)S(1)}, bf16[2048,256]{1,0:T(8,128)(2,1)S(1)}, u32[]{:S(2)}, u32[]{:S(2)}) collective-permute-start(bf16[2048,256]{1,0:T(8,128)(2,1)S(1)} %pad_maximum_fusion.2), channel_id=1, source_target_pairs={{0,8},{5,13},{10,2},{15,7},{16,24},{21,29},{26,18},{31,23}} | collective-permute-start | bytes 3145736 | tf_op jit(solution)/shard_map/ppermute | solution.py:21
  50.4 0.1 broadcast_select_fusion.2
  50.5 3.5 %collective-permute-start.9 = (bf16[1024,256]{1,0:T(8,128)(2,1)S(1)}, bf16[1024,256]{1,0:T(8,128)(2,1)S(1)}, u32[]{:S(2)}, u32[]{:S(2)}) collective-permute-start(bf16[1024,256]{1,0:T(8,128)(2,1)S(1)} %broadcast_select_fusion.2), channel_id=1, source_target_pairs={{0,16},{2,18},{5,21},{7,23},{8,24},{10,26},{13,29},{15,31},{16,0},... | collective-permute-start | bytes 1572872 | tf_op jit(solution)/shard_map/ppermute | solution.py:31
  53.9 0.1 broadcast_select_fusion.1
  54.0 2.5 %collective-permute-start.13 = (bf16[1024,256]{1,0:T(8,128)(2,1)S(1)}, bf16[1024,256]{1,0:T(8,128)(2,1)S(1)}, u32[]{:S(2)}, u32[]{:S(2)}) collective-permute-start(bf16[1024,256]{1,0:T(8,128)(2,1)S(1)} %broadcast_select_fusion.1), channel_id=1, source_target_pairs={{0,16},{2,18},{5,21},{7,23},{8,24},{10,26},{13,29},{15,31},{16,0},... | collective-permute-start | bytes 1572872 | tf_op jit(solution)/shard_map/ppermute | solution.py:31
  56.5 0.1 pad_maximum_fusion.refs_6_
  56.6 4.9 %collective-permute-done.9 = bf16[1024,256]{1,0:T(8,128)(2,1)S(1)} collective-permute-done((bf16[1024,256]{1,0:T(8,128)(2,1)S(1)}, bf16[1024,256]{1,0:T(8,128)(2,1)S(1)}, u32[]{:S(2)}, u32[]{:S(2)}) %collective-permute-start.9) | collective-permute-done | bytes 524320 | tf_op jit(solution)/shard_map/ppermute | solution.py:31
  61.5 1.3 %collective-permute-start.14 = (bf16[2048,256]{1,0:T(8,128)(2,1)S(1)}, bf16[2048,256]{1,0:T(8,128)(2,1)S(1)}, u32[]{:S(2)}, u32[]{:S(2)}) collective-permute-start(bf16[2048,256]{1,0:T(8,128)(2,1)S(1)} %pad_maximum_fusion.refs_6_), channel_id=1, source_target_pairs={{0,4},{2,6},{5,1},{7,3},{8,12},{10,14},{13,9},{15,11},{16,20},{18,... | collective-permute-start | bytes 3145736 | tf_op jit(solution)/shard_map/ppermute | solution.py:53
  62.9 0.1 pad_maximum_fusion.1.refs_7_
  63.0 1.4 %collective-permute-start.15 = (bf16[2048,256]{1,0:T(8,128)(2,1)S(1)}, bf16[2048,256]{1,0:T(8,128)(2,1)S(1)}, u32[]{:S(2)}, u32[]{:S(2)}) collective-permute-start(bf16[2048,256]{1,0:T(8,128)(2,1)S(1)} %pad_maximum_fusion.1.refs_7_), channel_id=1, source_target_pairs={{0,4},{2,6},{5,1},{7,3},{8,12},{10,14},{13,9},{15,11},{16,20},{18,... | collective-permute-start | bytes 3145736 | tf_op jit(solution)/shard_map/ppermute | solution.py:53
  64.3 2.8 %collective-permute-done.13 = bf16[1024,256]{1,0:T(8,128)(2,1)S(1)} collective-permute-done((bf16[1024,256]{1,0:T(8,128)(2,1)S(1)}, bf16[1024,256]{1,0:T(8,128)(2,1)S(1)}, u32[]{:S(2)}, u32[]{:S(2)}) %collective-permute-start.13) | collective-permute-done | bytes 524320 | tf_op jit(solution)/shard_map/ppermute | solution.py:31
  67.1 0.1 pad_maximum_fusion.3.refs_9_
  67.2 0.0 copy-start.2
  67.2 0.0 copy-start.4
  67.3 0.1 broadcast_select_fusion.refs_8_
  67.4 1.4 %collective-permute-start.17 = (bf16[2048,256]{1,0:T(8,128)(2,1)S(1)}, bf16[2048,256]{1,0:T(8,128)(2,1)S(1)}, u32[]{:S(2)}, u32[]{:S(2)}) collective-permute-start(bf16[2048,256]{1,0:T(8,128)(2,1)S(1)} %pad_maximum_fusion.3.refs_9_), channel_id=1, source_target_pairs={{0,4},{2,6},{5,1},{7,3},{8,12},{10,14},{13,9},{15,11},{16,20},{18,... | collective-permute-start | bytes 3145736 | tf_op jit(solution)/shard_map/ppermute | solution.py:53
  68.8 1.4 %collective-permute-start.16 = (bf16[2048,256]{1,0:T(8,128)(2,1)S(1)}, bf16[2048,256]{1,0:T(8,128)(2,1)S(1)}, u32[]{:S(2)}, u32[]{:S(2)}) collective-permute-start(bf16[2048,256]{1,0:T(8,128)(2,1)S(1)} %broadcast_select_fusion.refs_8_), channel_id=1, source_target_pairs={{0,4},{2,6},{5,1},{7,3},{8,12},{10,14},{13,9},{15,11},{16,20},{18,... | collective-permute-start | bytes 3145736 | tf_op jit(solution)/shard_map/ppermute | solution.py:53
  70.1 0.8 collective-permute-done.17.refs_13_
  71.0 1.5 %collective-permute-done.16.refs_12_ = bf16[2048,256]{1,0:T(8,128)(2,1)S(1)} collective-permute-done((bf16[2048,256]{1,0:T(8,128)(2,1)S(1)}, bf16[2048,256]{1,0:T(8,128)(2,1)S(1)}, u32[]{:S(2)}, u32[]{:S(2)}) %collective-permute-start.16) | collective-permute-done | bytes 1048608 | tf_op jit(solution)/shard_map/ppermute | solution.py:53
  72.5 2.9 %shard_map.77 = bf16[8,256,256]{2,1,0:T(8,128)(2,1)S(1)} custom-call(s32[8]{0:T(128)S(1)} %copy-done.4, s32[2,272]{1,0:T(2,128)S(1)} %bitcast.3, bf16[1024,256]{1,0:T(8,128)(2,1)S(1)} %get-tuple-element.14.refs_0_, bf16[1024,256]{1,0:T(8,128)(2,1)S(1)} %collective-permute-done.refs_1_, bf16[1024,256]{1,0:T(8,128)(2,1)S(1)} %collective-permute-done.1.refs_2_, ...), custom_call_target="tpu_custom_call" | custom-call | flops 268435456 | bytes 8388608 | tf_op jit(solution)/shard_map/pallas_call | solution.py:194
  75.4 0.5 collective-permute-start.18
  75.9 24.4 %shard_map.78.held = bf16[264,256,256]{2,1,0:T(8,128)(2,1)} custom-call(s32[264]{0:T(512)S(1)} %copy-done.3, s32[2,272]{1,0:T(2,128)S(1)} %bitcast.4, bf16[1024,256]{1,0:T(8,128)(2,1)S(1)} %get-tuple-element.14.refs_0_, bf16[1024,256]{1,0:T(8,128)(2,1)S(1)} %collective-permute-done.refs_1_, bf16[1024,256]{1,0:T(8,128)(2,1)S(1)} %collective-permute-done.1.refs_2_, ...), custom_call_target="tpu_custom_call" | custom-call | flops 8858370048 | bytes 75497472 | tf_op jit(solution)/shard_map/pallas_call | solution.py:194
  100.3 1.1 %collective-permute-done.18.incoming = bf16[8,256,256]{2,1,0:T(8,128)(2,1)S(1)} collective-permute-done((bf16[8,256,256]{2,1,0:T(8,128)(2,1)S(1)}, bf16[8,256,256]{2,1,0:T(8,128)(2,1)S(1)}, u32[]{:S(2)}, u32[]{:S(2)}) %collective-permute-start.18) | collective-permute-done | bytes 1048608 | tf_op jit(solution)/shard_map/ppermute | solution.py:275
  101.4 1.6 %shard_map.79 = bf16[264,256,256]{2,1,0:T(8,128)(2,1)} custom-call(s32[8]{0:T(128)S(1)} %select_reduce_fusion.places, bf16[8,256,256]{2,1,0:T(8,128)(2,1)S(1)} %collective-permute-done.18.incoming, bf16[264,256,256]{2,1,0:T(8,128)(2,1)} %shard_map.78.held), custom_call_target="tpu_custom_call", output_to_operand_aliasing={{}: (2, {})} | custom-call | tf_op jit(solution)/shard_map/pallas_call | solution.py:236
  (19 shorter events, 0.0 us)
Async XLA Ops:
  0.6 1.2 %copy-start = (f32[1024,256]{1,0:T(8,128)S(1)}, f32[1024,256]{1,0:T(8,128)}, u32[]{:S(2)}) copy-start(f32[1024,256]{1,0:T(8,128)} %param.6) | copy-start | bytes 3145732
  4.4 11.5 %collective-permute-start.2 = (bf16[1024,256]{1,0:T(8,128)(2,1)S(1)}, bf16[1024,256]{1,0:T(8,128)(2,1)S(1)}, u32[]{:S(2)}, u32[]{:S(2)}) collective-permute-start(bf16[1024,256]{1,0:T(8,128)(2,1)S(1)} %get-tuple-element.14.refs_0_), channel_id=1, source_target_pairs={{0,8},{5,13},{10,2},{15,7},{16,24},{21,29},{26,18},{31,23}} | collective-permute-start | bytes 1572872 | tf_op jit(solution)/shard_map/ppermute | solution.py:21
  9.3 23.1 %collective-permute-start.1 = (bf16[1024,256]{1,0:T(8,128)(2,1)S(1)}, bf16[1024,256]{1,0:T(8,128)(2,1)S(1)}, u32[]{:S(2)}, u32[]{:S(2)}) collective-permute-start(bf16[1024,256]{1,0:T(8,128)(2,1)S(1)} %get-tuple-element.14.refs_0_), channel_id=1, source_target_pairs={{0,2},{1,3},{2,0},{3,1},{4,6},{5,7},{6,4},{7,5},{8,10},{9,11},{10,... | collective-permute-start | bytes 1572872 | tf_op jit(solution)/shard_map/ppermute | solution.py:65
  9.8 23.3 %collective-permute-start = (bf16[1024,256]{1,0:T(8,128)(2,1)S(1)}, bf16[1024,256]{1,0:T(8,128)(2,1)S(1)}, u32[]{:S(2)}, u32[]{:S(2)}) collective-permute-start(bf16[1024,256]{1,0:T(8,128)(2,1)S(1)} %get-tuple-element.14.refs_0_), channel_id=1, source_target_pairs={{0,1},{1,0},{2,3},{3,2},{4,5},{5,4},{6,7},{7,6},{8,9},{9,8},{10,11... | collective-permute-start | bytes 1572872 | tf_op jit(solution)/shard_map/ppermute | solution.py:65
  16.0 17.1 %collective-permute-start.3 = (bf16[1024,256]{1,0:T(8,128)(2,1)S(1)}, bf16[1024,256]{1,0:T(8,128)(2,1)S(1)}, u32[]{:S(2)}, u32[]{:S(2)}) collective-permute-start(bf16[1024,256]{1,0:T(8,128)(2,1)S(1)} %broadcast_select_fusion.3), channel_id=1, source_target_pairs={{0,16},{2,18},{5,21},{7,23},{8,24},{10,26},{13,29},{15,31},{16,0},... | collective-permute-start | bytes 1572872 | tf_op jit(solution)/shard_map/ppermute | solution.py:31
  32.4 7.6 %collective-permute-start.5 = (bf16[1024,256]{1,0:T(8,128)(2,1)S(1)}, bf16[1024,256]{1,0:T(8,128)(2,1)S(1)}, u32[]{:S(2)}, u32[]{:S(2)}) collective-permute-start(bf16[1024,256]{1,0:T(8,128)(2,1)S(1)} %get-tuple-element.14.refs_0_), channel_id=1, source_target_pairs={{6,5},{9,10},{22,21},{25,26}} | collective-permute-start | bytes 1572872 | tf_op jit(solution)/shard_map/ppermute | solution.py:71
  33.1 0.8 copy-start.5
  33.9 11.1 %collective-permute-start.4 = (bf16[1024,256]{1,0:T(8,128)(2,1)S(1)}, bf16[1024,256]{1,0:T(8,128)(2,1)S(1)}, u32[]{:S(2)}, u32[]{:S(2)}) collective-permute-start(bf16[1024,256]{1,0:T(8,128)(2,1)S(1)} %collective-permute-done.1.refs_2_), channel_id=1, source_target_pairs={{1,0},{14,15},{17,16},{30,31}} | collective-permute-start | bytes 1572872 | tf_op jit(solution)/shard_map/ppermute | solution.py:72
  35.2 12.6 %collective-permute-start.10 = (bf16[1024,256]{1,0:T(8,128)(2,1)S(1)}, bf16[1024,256]{1,0:T(8,128)(2,1)}, u32[]{:S(2)}, u32[]{:S(2)}) collective-permute-start(bf16[1024,256]{1,0:T(8,128)(2,1)S(1)} %collective-permute-done.1.refs_2_), channel_id=1, source_target_pairs={{0,16},{5,21},{10,26},{15,31},{16,0},{21,5},{26,10},{31,15}} | collective-permute-start | bytes 1572872 | tf_op jit(solution)/shard_map/ppermute | solution.py:31
  38.7 11.7 %collective-permute-start.8 = (bf16[1024,256]{1,0:T(8,128)(2,1)S(1)}, bf16[1024,256]{1,0:T(8,128)(2,1)S(1)}, u32[]{:S(2)}, u32[]{:S(2)}) collective-permute-start(bf16[1024,256]{1,0:T(8,128)(2,1)S(1)} %collective-permute-done.refs_1_), channel_id=1, source_target_pairs={{0,8},{5,13},{10,2},{15,7},{16,24},{21,29},{26,18},{31,23}} | collective-permute-start | bytes 1572872 | tf_op jit(solution)/shard_map/ppermute | solution.py:21
  45.0 8.9 %collective-permute-start.12 = (bf16[1024,256]{1,0:T(8,128)(2,1)S(1)}, bf16[1024,256]{1,0:T(8,128)(2,1)S(1)}, u32[]{:S(2)}, u32[]{:S(2)}) collective-permute-start(bf16[1024,256]{1,0:T(8,128)(2,1)S(1)} %broadcast_select_fusion.4.refs_3_), channel_id=1, source_target_pairs={{0,8},{5,13},{10,2},{15,7},{16,24},{21,29},{26,18},{31,23}} | collective-permute-start | bytes 1572872 | tf_op jit(solution)/shard_map/ppermute | solution.py:21
  46.3 16.6 %collective-permute-start.6 = (bf16[1024,256]{1,0:T(8,128)(2,1)S(1)}, bf16[1024,256]{1,0:T(8,128)(2,1)S(1)}, u32[]{:S(2)}, u32[]{:S(2)}) collective-permute-start(bf16[1024,256]{1,0:T(8,128)(2,1)S(1)} %collective-permute-done.1.refs_2_), channel_id=1, source_target_pairs={{2,3},{5,4},{6,7},{9,8},{10,11},{13,12},{18,19},{21,20},{22,23},{2... | collective-permute-start | bytes 1572872 | tf_op jit(solution)/shard_map/ppermute | solution.py:77
  47.0 15.9 %collective-permute-start.7 = (bf16[1024,256]{1,0:T(8,128)(2,1)S(1)}, bf16[1024,256]{1,0:T(8,128)(2,1)S(1)}, u32[]{:S(2)}, u32[]{:S(2)}) collective-permute-start(bf16[1024,256]{1,0:T(8,128)(2,1)S(1)} %get-tuple-element.14.refs_0_), channel_id=1, source_target_pairs={{1,2},{2,1},{5,6},{10,9},{13,14},{14,13},{17,18},{18,17},{21,22},{... | collective-permute-start | bytes 1572872 | tf_op jit(solution)/shard_map/ppermute | solution.py:76
  48.9 7.7 %copy-start.6 = (bf16[1024,256]{1,0:T(8,128)(2,1)S(1)}, bf16[1024,256]{1,0:T(8,128)(2,1)}, u32[]{:S(2)}) copy-start(bf16[1024,256]{1,0:T(8,128)(2,1)} %copy-done.5) | copy-start | bytes 1572868
  48.9 18.4 %collective-permute-start.11 = (bf16[2048,256]{1,0:T(8,128)(2,1)S(1)}, bf16[2048,256]{1,0:T(8,128)(2,1)S(1)}, u32[]{:S(2)}, u32[]{:S(2)}) collective-permute-start(bf16[2048,256]{1,0:T(8,128)(2,1)S(1)} %pad_maximum_fusion.2), channel_id=1, source_target_pairs={{0,8},{5,13},{10,2},{15,7},{16,24},{21,29},{26,18},{31,23}} | collective-permute-start | bytes 3145736 | tf_op jit(solution)/shard_map/ppermute | solution.py:21
  50.5 11.1 %collective-permute-start.9 = (bf16[1024,256]{1,0:T(8,128)(2,1)S(1)}, bf16[1024,256]{1,0:T(8,128)(2,1)S(1)}, u32[]{:S(2)}, u32[]{:S(2)}) collective-permute-start(bf16[1024,256]{1,0:T(8,128)(2,1)S(1)} %broadcast_select_fusion.2), channel_id=1, source_target_pairs={{0,16},{2,18},{5,21},{7,23},{8,24},{10,26},{13,29},{15,31},{16,0},... | collective-permute-start | bytes 1572872 | tf_op jit(solution)/shard_map/ppermute | solution.py:31
  54.0 13.1 %collective-permute-start.13 = (bf16[1024,256]{1,0:T(8,128)(2,1)S(1)}, bf16[1024,256]{1,0:T(8,128)(2,1)S(1)}, u32[]{:S(2)}, u32[]{:S(2)}) collective-permute-start(bf16[1024,256]{1,0:T(8,128)(2,1)S(1)} %broadcast_select_fusion.1), channel_id=1, source_target_pairs={{0,16},{2,18},{5,21},{7,23},{8,24},{10,26},{13,29},{15,31},{16,0},... | collective-permute-start | bytes 1572872 | tf_op jit(solution)/shard_map/ppermute | solution.py:31
  61.5 8.6 %collective-permute-start.14 = (bf16[2048,256]{1,0:T(8,128)(2,1)S(1)}, bf16[2048,256]{1,0:T(8,128)(2,1)S(1)}, u32[]{:S(2)}, u32[]{:S(2)}) collective-permute-start(bf16[2048,256]{1,0:T(8,128)(2,1)S(1)} %pad_maximum_fusion.refs_6_), channel_id=1, source_target_pairs={{0,4},{2,6},{5,1},{7,3},{8,12},{10,14},{13,9},{15,11},{16,20},{18,... | collective-permute-start | bytes 3145736 | tf_op jit(solution)/shard_map/ppermute | solution.py:53
  63.0 7.2 %collective-permute-start.15 = (bf16[2048,256]{1,0:T(8,128)(2,1)S(1)}, bf16[2048,256]{1,0:T(8,128)(2,1)S(1)}, u32[]{:S(2)}, u32[]{:S(2)}) collective-permute-start(bf16[2048,256]{1,0:T(8,128)(2,1)S(1)} %pad_maximum_fusion.1.refs_7_), channel_id=1, source_target_pairs={{0,4},{2,6},{5,1},{7,3},{8,12},{10,14},{13,9},{15,11},{16,20},{18,... | collective-permute-start | bytes 3145736 | tf_op jit(solution)/shard_map/ppermute | solution.py:53
  67.2 5.2 %copy-start.2 = (s32[272,2]{0,1:T(2,128)S(1)}, s32[272,2]{0,1:T(2,128)}, u32[]{:S(2)}) copy-start(s32[272,2]{0,1:T(2,128)} %param.9) | copy-start | bytes 6532
  67.2 5.2 %copy-start.4 = (s32[8]{0:T(128)S(1)}, s32[8]{0:T(128)}, u32[]{:S(2)}) copy-start(s32[8]{0:T(128)} %source_list.2) | copy-start | bytes 100
  67.4 3.6 %collective-permute-start.17 = (bf16[2048,256]{1,0:T(8,128)(2,1)S(1)}, bf16[2048,256]{1,0:T(8,128)(2,1)S(1)}, u32[]{:S(2)}, u32[]{:S(2)}) collective-permute-start(bf16[2048,256]{1,0:T(8,128)(2,1)S(1)} %pad_maximum_fusion.3.refs_9_), channel_id=1, source_target_pairs={{0,4},{2,6},{5,1},{7,3},{8,12},{10,14},{13,9},{15,11},{16,20},{18,... | collective-permute-start | bytes 3145736 | tf_op jit(solution)/shard_map/ppermute | solution.py:53
  68.8 3.7 %collective-permute-start.16 = (bf16[2048,256]{1,0:T(8,128)(2,1)S(1)}, bf16[2048,256]{1,0:T(8,128)(2,1)S(1)}, u32[]{:S(2)}, u32[]{:S(2)}) collective-permute-start(bf16[2048,256]{1,0:T(8,128)(2,1)S(1)} %broadcast_select_fusion.refs_8_), channel_id=1, source_target_pairs={{0,4},{2,6},{5,1},{7,3},{8,12},{10,14},{13,9},{15,11},{16,20},{18,... | collective-permute-start | bytes 3145736 | tf_op jit(solution)/shard_map/ppermute | solution.py:53
  72.5 3.4 %copy-start.3 = (s32[264]{0:T(512)S(1)}, s32[264]{0:T(512)}, u32[]{:S(2)}) copy-start(s32[264]{0:T(512)} %source_list.3) | copy-start | bytes 3172
  75.4 26.0 %collective-permute-start.18 = (bf16[8,256,256]{2,1,0:T(8,128)(2,1)S(1)}, bf16[8,256,256]{2,1,0:T(8,128)(2,1)S(1)}, u32[]{:S(2)}, u32[]{:S(2)}) collective-permute-start(bf16[8,256,256]{2,1,0:T(8,128)(2,1)S(1)} %shard_map.77), channel_id=1, source_target_pairs={{0,28},{4,24},{8,20},{12,16},{16,12},{20,8},{24,4},{28,0},{1,29},{... | collective-permute-start | bytes 3145736 | tf_op jit(solution)/shard_map/ppermute | solution.py:275
  101.4 1.6 %copy-start.1 = (f32[1024,256]{1,0:T(8,128)S(1)}, f32[1024,256]{1,0:T(8,128)}, u32[]{:S(2)}) copy-start(f32[1024,256]{1,0:T(8,128)} %param.6) | copy-start | bytes 3145732

commit v2 on v1

--- a/solution.py
+++ b/solution.py
@@ -69,9 +69,9 @@
         at_end = (column == 0) | (column == 3)
         near = [jnp.concatenate(pieces[0], 0)]
         middle = lax.ppermute(tied(half, parts[2]), AXES, z_pairs(inner, True))
-        onward = lax.ppermute(tied(parts[2], pieces[0][-1], parts[1]), AXES, z_pairs(outer, True))
+        onward = lax.ppermute(parts[2], AXES, z_pairs(outer, True))
         first = jnp.where(at_end, onward, middle)
-        turned = jnp.concatenate(exchanged(parts[2], col_count - 1, *sizes), 0)
+        turned = jnp.concatenate(exchanged(tied(parts[2], parts[1], pieces[0][-1]), col_count - 1, *sizes), 0)
         pieces.append(forward(parts[1]))
         middle = lax.ppermute(tied(half, parts[1], parts[2]), AXES, z_pairs(inner, False))
         onward = lax.ppermute(tied(parts[2], parts[1]), AXES, z_pairs(outer, False))

time: 104 us -> 103 us (level)
  no operation moved by 1% of the time
where the time goes in v2:
time: 103 us; the launch traced here: 102 us
  waiting for transfers between devices  33.2 us (32%)
  starting transfers between devices  32.6 us (32%)
  Pallas kernels  29 us (28%)
  other arithmetic  2.67 us (3%)
  matrix products  2.54 us (2%)
  local copies, waits for them, and re-layouts  1.09 us (1%)
    pallas_call x2, Pallas kernels, renew(): pl.pallas_call(functools.partial(renew_kernel, sizes), out_shape=jax.Shap...  27.4 us
    ppermute x2, waiting for transfers between devices, gather_and_spread(): lax.ppermute(half, 'col', [(place, place ^ mask) for place in range(col_c...  12.9 us
    ppermute x4, starting transfers between devices, exchanged(): lax.ppermute(piece, AXES, spread_pairs(bit, known, row_count, col_count))  12.9 us
    ppermute x4, starting transfers between devices, across(): lax.ppermute(value, AXES, spread_pairs(bit, known, row_count, col_count))  9 us
    ppermute x4, waiting for transfers between devices, exchanged(): lax.ppermute(piece, AXES, spread_pairs(bit, known, row_count, col_count))  7.72 us
    ppermute x4, starting transfers between devices, to_other_core(): return lax.ppermute(near, AXES, spread_pairs(0, 1, *sizes))  5.41 us
    ppermute x4, waiting for transfers between devices, across(): lax.ppermute(value, AXES, spread_pairs(bit, known, row_count, col_count))  5.16 us
    ppermute x1, waiting for transfers between devices, gather_and_spread(): onward = lax.ppermute(parts[2], AXES, z_pairs(outer, True))  4.13 us
  transfers between devices with their start and end apart: 19, of which 8 were waited for; matrix products, arithmetic and copies ran while one was open for 2% of the time, Pallas kernels for 24%

profile of v2, /device:TPU:0, one launch (start us, length us, event | category | flops | bytes accessed | tf_op | source)
XLA Modules:
  0.0 102.1 jit_solution(9964184265028635594)
XLA Ops:
  0.6 0.0 copy-start
  0.7 1.0 select_reduce_fusion.places
  1.6 0.3 copy-done
  1.9 2.5 %fusion = (bf16[1024,256]{1,0:T(8,128)(2,1)S(1)}, f32[1024,256]{1,0:T(8,128)}) fusion(f32[1024,256]{1,0:T(8,128)S(1)} %copy-done, f32[256,256]{1,0:T(8,128)} %param.7), kind=kOutput, calls=%fused_computation.11 | convolution fusion | flops 402915328 | bytes 2883584 | tf_op jit(solution)/shard_map/dot_general | solution.py:259
  4.4 4.9 %collective-permute-start.6 = (bf16[1024,256]{1,0:T(8,128)(2,1)S(1)}, bf16[1024,256]{1,0:T(8,128)(2,1)S(1)}, u32[]{:S(2)}, u32[]{:S(2)}) collective-permute-start(bf16[1024,256]{1,0:T(8,128)(2,1)S(1)} %get-tuple-element.13.refs_0_), channel_id=1, source_target_pairs={{0,8},{5,13},{10,2},{15,7},{16,24},{21,29},{26,18},{31,23}} | collective-permute-start | bytes 1572872 | tf_op jit(solution)/shard_map/ppermute | solution.py:21
  9.3 0.5 collective-permute-start.1
  9.8 1.0 collective-permute-start
  10.8 5.2 %collective-permute-done.6 = bf16[1024,256]{1,0:T(8,128)(2,1)S(1)} collective-permute-done((bf16[1024,256]{1,0:T(8,128)(2,1)S(1)}, bf16[1024,256]{1,0:T(8,128)(2,1)S(1)}, u32[]{:S(2)}, u32[]{:S(2)}) %collective-permute-start.6) | collective-permute-done | bytes 524320 | tf_op jit(solution)/shard_map/ppermute | solution.py:21
  15.9 0.1 broadcast_select_fusion.3
  16.0 3.4 %collective-permute-start.7 = (bf16[1024,256]{1,0:T(8,128)(2,1)S(1)}, bf16[1024,256]{1,0:T(8,128)(2,1)S(1)}, u32[]{:S(2)}, u32[]{:S(2)}) collective-permute-start(bf16[1024,256]{1,0:T(8,128)(2,1)S(1)} %broadcast_select_fusion.3), channel_id=1, source_target_pairs={{0,16},{2,18},{5,21},{7,23},{8,24},{10,26},{13,29},{15,31},{16,0},... | collective-permute-start | bytes 1572872 | tf_op jit(solution)/shard_map/ppermute | solution.py:31
  19.5 12.9 %collective-permute-done.1.refs_2_ = bf16[1024,256]{1,0:T(8,128)(2,1)S(1)} collective-permute-done((bf16[1024,256]{1,0:T(8,128)(2,1)S(1)}, bf16[1024,256]{1,0:T(8,128)(2,1)S(1)}, u32[]{:S(2)}, u32[]{:S(2)}) %collective-permute-start.1) | collective-permute-done | bytes 524320 | tf_op jit(solution)/shard_map/ppermute | solution.py:65
  32.4 0.7 collective-permute-start.3
  33.1 1.3 %collective-permute-start.2 = (bf16[1024,256]{1,0:T(8,128)(2,1)S(1)}, bf16[1024,256]{1,0:T(8,128)(2,1)S(1)}, u32[]{:S(2)}, u32[]{:S(2)}) collective-permute-start(bf16[1024,256]{1,0:T(8,128)(2,1)S(1)} %collective-permute-done.1.refs_2_), channel_id=1, source_target_pairs={{1,0},{14,15},{17,16},{30,31}} | collective-permute-start | bytes 1572872 | tf_op jit(solution)/shard_map/ppermute | solution.py:72
  34.4 0.0 copy-start.5
  34.4 0.8 copy-done.5
  35.2 3.5 %collective-permute-start.10 = (bf16[1024,256]{1,0:T(8,128)(2,1)S(1)}, bf16[1024,256]{1,0:T(8,128)(2,1)}, u32[]{:S(2)}, u32[]{:S(2)}) collective-permute-start(bf16[1024,256]{1,0:T(8,128)(2,1)S(1)} %collective-permute-done.1.refs_2_), channel_id=1, source_target_pairs={{0,16},{5,21},{10,26},{15,31},{16,0},{21,5},{26,10},{31,15}} | collective-permute-start | bytes 1572872 | tf_op jit(solution)/shard_map/ppermute | solution.py:31
  38.7 1.3 %collective-permute-start.8 = (bf16[1024,256]{1,0:T(8,128)(2,1)S(1)}, bf16[1024,256]{1,0:T(8,128)(2,1)S(1)}, u32[]{:S(2)}, u32[]{:S(2)}) collective-permute-start(bf16[1024,256]{1,0:T(8,128)(2,1)S(1)} %collective-permute-done.refs_1_), channel_id=1, source_target_pairs={{0,8},{5,13},{10,2},{15,7},{16,24},{21,29},{26,18},{31,23}} | collective-permute-start | bytes 1572872 | tf_op jit(solution)/shard_map/ppermute | solution.py:21
  40.0 4.1 %collective-permute-done.2 = bf16[1024,256]{1,0:T(8,128)(2,1)S(1)} collective-permute-done((bf16[1024,256]{1,0:T(8,128)(2,1)S(1)}, bf16[1024,256]{1,0:T(8,128)(2,1)S(1)}, u32[]{:S(2)}, u32[]{:S(2)}) %collective-permute-start.2) | collective-permute-done | bytes 524320 | tf_op jit(solution)/shard_map/ppermute | solution.py:72
  44.1 0.1 broadcast_select_fusion.4.refs_3_
  44.2 1.3 %collective-permute-start.12 = (bf16[1024,256]{1,0:T(8,128)(2,1)S(1)}, bf16[1024,256]{1,0:T(8,128)(2,1)S(1)}, u32[]{:S(2)}, u32[]{:S(2)}) collective-permute-start(bf16[1024,256]{1,0:T(8,128)(2,1)S(1)} %broadcast_select_fusion.4.refs_3_), channel_id=1, source_target_pairs={{0,8},{5,13},{10,2},{15,7},{16,24},{21,29},{26,18},{31,23}} | collective-permute-start | bytes 1572872 | tf_op jit(solution)/shard_map/ppermute | solution.py:21
  45.5 0.7 collective-permute-start.4
  46.2 0.7 collective-permute-start.5
  46.9 1.1 %pad_maximum_fusion.2 = bf16[2048,256]{1,0:T(8,128)(2,1)S(1)} fusion(bf16[1024,256]{1,0:T(8,128)(2,1)} %collective-permute-done.10, bf16[1024,256]{1,0:T(8,128)(2,1)S(1)} %collective-permute-done.1.refs_2_), kind=kLoop, calls=%fused_computation.2 | loop fusion | flops 2097152 | bytes 2097152 | tf_op jit(solution)/shard_map/concatenate | solution.py:74
  48.1 0.0 copy-start.6
  48.1 1.5 %collective-permute-start.11 = (bf16[2048,256]{1,0:T(8,128)(2,1)S(1)}, bf16[2048,256]{1,0:T(8,128)(2,1)S(1)}, u32[]{:S(2)}, u32[]{:S(2)}) collective-permute-start(bf16[2048,256]{1,0:T(8,128)(2,1)S(1)} %pad_maximum_fusion.2), channel_id=1, source_target_pairs={{0,8},{5,13},{10,2},{15,7},{16,24},{21,29},{26,18},{31,23}} | collective-permute-start | bytes 3145736 | tf_op jit(solution)/shard_map/ppermute | solution.py:21
  49.6 0.1 broadcast_select_fusion.2
  49.6 3.5 %collective-permute-start.9 = (bf16[1024,256]{1,0:T(8,128)(2,1)S(1)}, bf16[1024,256]{1,0:T(8,128)(2,1)S(1)}, u32[]{:S(2)}, u32[]{:S(2)}) collective-permute-start(bf16[1024,256]{1,0:T(8,128)(2,1)S(1)} %broadcast_select_fusion.2), channel_id=1, source_target_pairs={{0,16},{2,18},{5,21},{7,23},{8,24},{10,26},{13,29},{15,31},{16,0},... | collective-permute-start | bytes 1572872 | tf_op jit(solution)/shard_map/ppermute | solution.py:31
  53.1 0.1 broadcast_select_fusion.1
  53.2 2.5 %collective-permute-start.13 = (bf16[1024,256]{1,0:T(8,128)(2,1)S(1)}, bf16[1024,256]{1,0:T(8,128)(2,1)S(1)}, u32[]{:S(2)}, u32[]{:S(2)}) collective-permute-start(bf16[1024,256]{1,0:T(8,128)(2,1)S(1)} %broadcast_select_fusion.1), channel_id=1, source_target_pairs={{0,16},{2,18},{5,21},{7,23},{8,24},{10,26},{13,29},{15,31},{16,0},... | collective-permute-start | bytes 1572872 | tf_op jit(solution)/shard_map/ppermute | solution.py:31
  55.7 0.1 pad_maximum_fusion.refs_6_
  55.8 4.9 %collective-permute-done.9 = bf16[1024,256]{1,0:T(8,128)(2,1)S(1)} collective-permute-done((bf16[1024,256]{1,0:T(8,128)(2,1)S(1)}, bf16[1024,256]{1,0:T(8,128)(2,1)S(1)}, u32[]{:S(2)}, u32[]{:S(2)}) %collective-permute-start.9) | collective-permute-done | bytes 524320 | tf_op jit(solution)/shard_map/ppermute | solution.py:31
  60.7 1.3 %collective-permute-start.14 = (bf16[2048,256]{1,0:T(8,128)(2,1)S(1)}, bf16[2048,256]{1,0:T(8,128)(2,1)S(1)}, u32[]{:S(2)}, u32[]{:S(2)}) collective-permute-start(bf16[2048,256]{1,0:T(8,128)(2,1)S(1)} %pad_maximum_fusion.refs_6_), channel_id=1, source_target_pairs={{0,4},{2,6},{5,1},{7,3},{8,12},{10,14},{13,9},{15,11},{16,20},{18,... | collective-permute-start | bytes 3145736 | tf_op jit(solution)/shard_map/ppermute | solution.py:53
  62.1 0.1 pad_maximum_fusion.1.refs_7_
  62.2 1.4 %collective-permute-start.15 = (bf16[2048,256]{1,0:T(8,128)(2,1)S(1)}, bf16[2048,256]{1,0:T(8,128)(2,1)S(1)}, u32[]{:S(2)}, u32[]{:S(2)}) collective-permute-start(bf16[2048,256]{1,0:T(8,128)(2,1)S(1)} %pad_maximum_fusion.1.refs_7_), channel_id=1, source_target_pairs={{0,4},{2,6},{5,1},{7,3},{8,12},{10,14},{13,9},{15,11},{16,20},{18,... | collective-permute-start | bytes 3145736 | tf_op jit(solution)/shard_map/ppermute | solution.py:53
  63.5 2.8 %collective-permute-done.13 = bf16[1024,256]{1,0:T(8,128)(2,1)S(1)} collective-permute-done((bf16[1024,256]{1,0:T(8,128)(2,1)S(1)}, bf16[1024,256]{1,0:T(8,128)(2,1)S(1)}, u32[]{:S(2)}, u32[]{:S(2)}) %collective-permute-start.13) | collective-permute-done | bytes 524320 | tf_op jit(solution)/shard_map/ppermute | solution.py:31
  66.3 0.1 pad_maximum_fusion.3.refs_9_
  66.4 0.0 copy-start.2
  66.4 0.0 copy-start.4
  66.4 0.1 broadcast_select_fusion.refs_8_
  66.6 1.4 %collective-permute-start.17 = (bf16[2048,256]{1,0:T(8,128)(2,1)S(1)}, bf16[2048,256]{1,0:T(8,128)(2,1)S(1)}, u32[]{:S(2)}, u32[]{:S(2)}) collective-permute-start(bf16[2048,256]{1,0:T(8,128)(2,1)S(1)} %pad_maximum_fusion.3.refs_9_), channel_id=1, source_target_pairs={{0,4},{2,6},{5,1},{7,3},{8,12},{10,14},{13,9},{15,11},{16,20},{18,... | collective-permute-start | bytes 3145736 | tf_op jit(solution)/shard_map/ppermute | solution.py:53
  68.0 1.4 %collective-permute-start.16 = (bf16[2048,256]{1,0:T(8,128)(2,1)S(1)}, bf16[2048,256]{1,0:T(8,128)(2,1)S(1)}, u32[]{:S(2)}, u32[]{:S(2)}) collective-permute-start(bf16[2048,256]{1,0:T(8,128)(2,1)S(1)} %broadcast_select_fusion.refs_8_), channel_id=1, source_target_pairs={{0,4},{2,6},{5,1},{7,3},{8,12},{10,14},{13,9},{15,11},{16,20},{18,... | collective-permute-start | bytes 3145736 | tf_op jit(solution)/shard_map/ppermute | solution.py:53
  69.3 0.8 collective-permute-done.17.refs_13_
  70.2 1.5 %collective-permute-done.16.refs_12_ = bf16[2048,256]{1,0:T(8,128)(2,1)S(1)} collective-permute-done((bf16[2048,256]{1,0:T(8,128)(2,1)S(1)}, bf16[2048,256]{1,0:T(8,128)(2,1)S(1)}, u32[]{:S(2)}, u32[]{:S(2)}) %collective-permute-start.16) | collective-permute-done | bytes 1048608 | tf_op jit(solution)/shard_map/ppermute | solution.py:53
  71.7 2.9 %shard_map.77 = bf16[8,256,256]{2,1,0:T(8,128)(2,1)S(1)} custom-call(s32[8]{0:T(128)S(1)} %copy-done.4, s32[2,272]{1,0:T(2,128)S(1)} %bitcast.3, bf16[1024,256]{1,0:T(8,128)(2,1)S(1)} %get-tuple-element.13.refs_0_, bf16[1024,256]{1,0:T(8,128)(2,1)S(1)} %collective-permute-done.refs_1_, bf16[1024,256]{1,0:T(8,128)(2,1)S(1)} %collective-permute-done.1.refs_2_, ...), custom_call_target="tpu_custom_call" | custom-call | flops 268435456 | bytes 8388608 | tf_op jit(solution)/shard_map/pallas_call | solution.py:194
  74.6 0.5 collective-permute-start.18
  75.1 24.5 %shard_map.78.held = bf16[264,256,256]{2,1,0:T(8,128)(2,1)} custom-call(s32[264]{0:T(512)S(1)} %copy-done.3, s32[2,272]{1,0:T(2,128)S(1)} %bitcast.4, bf16[1024,256]{1,0:T(8,128)(2,1)S(1)} %get-tuple-element.13.refs_0_, bf16[1024,256]{1,0:T(8,128)(2,1)S(1)} %collective-permute-done.refs_1_, bf16[1024,256]{1,0:T(8,128)(2,1)S(1)} %collective-permute-done.1.refs_2_, ...), custom_call_target="tpu_custom_call" | custom-call | flops 8858370048 | bytes 75497472 | tf_op jit(solution)/shard_map/pallas_call | solution.py:194
  99.6 1.0 collective-permute-done.18.incoming
  100.6 1.6 %shard_map.79 = bf16[264,256,256]{2,1,0:T(8,128)(2,1)} custom-call(s32[8]{0:T(128)S(1)} %select_reduce_fusion.places, bf16[8,256,256]{2,1,0:T(8,128)(2,1)S(1)} %collective-permute-done.18.incoming, bf16[264,256,256]{2,1,0:T(8,128)(2,1)} %shard_map.78.held), custom_call_target="tpu_custom_call", output_to_operand_aliasing={{}: (2, {})} | custom-call | tf_op jit(solution)/shard_map/pallas_call | solution.py:236
  (19 shorter events, 0.0 us)
Async XLA Ops:
  0.6 1.2 %copy-start = (f32[1024,256]{1,0:T(8,128)S(1)}, f32[1024,256]{1,0:T(8,128)}, u32[]{:S(2)}) copy-start(f32[1024,256]{1,0:T(8,128)} %param.6) | copy-start | bytes 3145732
  4.4 11.5 %collective-permute-start.6 = (bf16[1024,256]{1,0:T(8,128)(2,1)S(1)}, bf16[1024,256]{1,0:T(8,128)(2,1)S(1)}, u32[]{:S(2)}, u32[]{:S(2)}) collective-permute-start(bf16[1024,256]{1,0:T(8,128)(2,1)S(1)} %get-tuple-element.13.refs_0_), channel_id=1, source_target_pairs={{0,8},{5,13},{10,2},{15,7},{16,24},{21,29},{26,18},{31,23}} | collective-permute-start | bytes 1572872 | tf_op jit(solution)/shard_map/ppermute | solution.py:21
  9.3 23.1 %collective-permute-start.1 = (bf16[1024,256]{1,0:T(8,128)(2,1)S(1)}, bf16[1024,256]{1,0:T(8,128)(2,1)S(1)}, u32[]{:S(2)}, u32[]{:S(2)}) collective-permute-start(bf16[1024,256]{1,0:T(8,128)(2,1)S(1)} %get-tuple-element.13.refs_0_), channel_id=1, source_target_pairs={{0,2},{1,3},{2,0},{3,1},{4,6},{5,7},{6,4},{7,5},{8,10},{9,11},{10,... | collective-permute-start | bytes 1572872 | tf_op jit(solution)/shard_map/ppermute | solution.py:65
  9.8 24.6 %collective-permute-start = (bf16[1024,256]{1,0:T(8,128)(2,1)S(1)}, bf16[1024,256]{1,0:T(8,128)(2,1)S(1)}, u32[]{:S(2)}, u32[]{:S(2)}) collective-permute-start(bf16[1024,256]{1,0:T(8,128)(2,1)S(1)} %get-tuple-element.13.refs_0_), channel_id=1, source_target_pairs={{0,1},{1,0},{2,3},{3,2},{4,5},{5,4},{6,7},{7,6},{8,9},{9,8},{10,11... | collective-permute-start | bytes 1572872 | tf_op jit(solution)/shard_map/ppermute | solution.py:65
  16.0 18.4 %collective-permute-start.7 = (bf16[1024,256]{1,0:T(8,128)(2,1)S(1)}, bf16[1024,256]{1,0:T(8,128)(2,1)S(1)}, u32[]{:S(2)}, u32[]{:S(2)}) collective-permute-start(bf16[1024,256]{1,0:T(8,128)(2,1)S(1)} %broadcast_select_fusion.3), channel_id=1, source_target_pairs={{0,16},{2,18},{5,21},{7,23},{8,24},{10,26},{13,29},{15,31},{16,0},... | collective-permute-start | bytes 1572872 | tf_op jit(solution)/shard_map/ppermute | solution.py:31
  32.4 7.6 %collective-permute-start.3 = (bf16[1024,256]{1,0:T(8,128)(2,1)S(1)}, bf16[1024,256]{1,0:T(8,128)(2,1)S(1)}, u32[]{:S(2)}, u32[]{:S(2)}) collective-permute-start(bf16[1024,256]{1,0:T(8,128)(2,1)S(1)} %get-tuple-element.13.refs_0_), channel_id=1, source_target_pairs={{6,5},{9,10},{22,21},{25,26}} | collective-permute-start | bytes 1572872 | tf_op jit(solution)/shard_map/ppermute | solution.py:71
  33.1 11.1 %collective-permute-start.2 = (bf16[1024,256]{1,0:T(8,128)(2,1)S(1)}, bf16[1024,256]{1,0:T(8,128)(2,1)S(1)}, u32[]{:S(2)}, u32[]{:S(2)}) collective-permute-start(bf16[1024,256]{1,0:T(8,128)(2,1)S(1)} %collective-permute-done.1.refs_2_), channel_id=1, source_target_pairs={{1,0},{14,15},{17,16},{30,31}} | collective-permute-start | bytes 1572872 | tf_op jit(solution)/shard_map/ppermute | solution.py:72
  34.4 0.8 copy-start.5
  35.2 11.8 %collective-permute-start.10 = (bf16[1024,256]{1,0:T(8,128)(2,1)S(1)}, bf16[1024,256]{1,0:T(8,128)(2,1)}, u32[]{:S(2)}, u32[]{:S(2)}) collective-permute-start(bf16[1024,256]{1,0:T(8,128)(2,1)S(1)} %collective-permute-done.1.refs_2_), channel_id=1, source_target_pairs={{0,16},{5,21},{10,26},{15,31},{16,0},{21,5},{26,10},{31,15}} | collective-permute-start | bytes 1572872 | tf_op jit(solution)/shard_map/ppermute | solution.py:31
  38.7 10.9 %collective-permute-start.8 = (bf16[1024,256]{1,0:T(8,128)(2,1)S(1)}, bf16[1024,256]{1,0:T(8,128)(2,1)S(1)}, u32[]{:S(2)}, u32[]{:S(2)}) collective-permute-start(bf16[1024,256]{1,0:T(8,128)(2,1)S(1)} %collective-permute-done.refs_1_), channel_id=1, source_target_pairs={{0,8},{5,13},{10,2},{15,7},{16,24},{21,29},{26,18},{31,23}} | collective-permute-start | bytes 1572872 | tf_op jit(solution)/shard_map/ppermute | solution.py:21
  44.2 8.9 %collective-permute-start.12 = (bf16[1024,256]{1,0:T(8,128)(2,1)S(1)}, bf16[1024,256]{1,0:T(8,128)(2,1)S(1)}, u32[]{:S(2)}, u32[]{:S(2)}) collective-permute-start(bf16[1024,256]{1,0:T(8,128)(2,1)S(1)} %broadcast_select_fusion.4.refs_3_), channel_id=1, source_target_pairs={{0,8},{5,13},{10,2},{15,7},{16,24},{21,29},{26,18},{31,23}} | collective-permute-start | bytes 1572872 | tf_op jit(solution)/shard_map/ppermute | solution.py:21
  45.5 16.6 %collective-permute-start.4 = (bf16[1024,256]{1,0:T(8,128)(2,1)S(1)}, bf16[1024,256]{1,0:T(8,128)(2,1)S(1)}, u32[]{:S(2)}, u32[]{:S(2)}) collective-permute-start(bf16[1024,256]{1,0:T(8,128)(2,1)S(1)} %collective-permute-done.1.refs_2_), channel_id=1, source_target_pairs={{2,3},{5,4},{6,7},{9,8},{10,11},{13,12},{18,19},{21,20},{22,23},{2... | collective-permute-start | bytes 1572872 | tf_op jit(solution)/shard_map/ppermute | solution.py:77
  46.2 15.9 %collective-permute-start.5 = (bf16[1024,256]{1,0:T(8,128)(2,1)S(1)}, bf16[1024,256]{1,0:T(8,128)(2,1)S(1)}, u32[]{:S(2)}, u32[]{:S(2)}) collective-permute-start(bf16[1024,256]{1,0:T(8,128)(2,1)S(1)} %get-tuple-element.13.refs_0_), channel_id=1, source_target_pairs={{1,2},{2,1},{5,6},{10,9},{13,14},{14,13},{17,18},{18,17},{21,22},{... | collective-permute-start | bytes 1572872 | tf_op jit(solution)/shard_map/ppermute | solution.py:76
  48.1 7.7 %copy-start.6 = (bf16[1024,256]{1,0:T(8,128)(2,1)S(1)}, bf16[1024,256]{1,0:T(8,128)(2,1)}, u32[]{:S(2)}) copy-start(bf16[1024,256]{1,0:T(8,128)(2,1)} %copy-done.5) | copy-start | bytes 1572868
  48.1 18.4 %collective-permute-start.11 = (bf16[2048,256]{1,0:T(8,128)(2,1)S(1)}, bf16[2048,256]{1,0:T(8,128)(2,1)S(1)}, u32[]{:S(2)}, u32[]{:S(2)}) collective-permute-start(bf16[2048,256]{1,0:T(8,128)(2,1)S(1)} %pad_maximum_fusion.2), channel_id=1, source_target_pairs={{0,8},{5,13},{10,2},{15,7},{16,24},{21,29},{26,18},{31,23}} | collective-permute-start | bytes 3145736 | tf_op jit(solution)/shard_map/ppermute | solution.py:21
  49.6 11.1 %collective-permute-start.9 = (bf16[1024,256]{1,0:T(8,128)(2,1)S(1)}, bf16[1024,256]{1,0:T(8,128)(2,1)S(1)}, u32[]{:S(2)}, u32[]{:S(2)}) collective-permute-start(bf16[1024,256]{1,0:T(8,128)(2,1)S(1)} %broadcast_select_fusion.2), channel_id=1, source_target_pairs={{0,16},{2,18},{5,21},{7,23},{8,24},{10,26},{13,29},{15,31},{16,0},... | collective-permute-start | bytes 1572872 | tf_op jit(solution)/shard_map/ppermute | solution.py:31
  53.2 13.1 %collective-permute-start.13 = (bf16[1024,256]{1,0:T(8,128)(2,1)S(1)}, bf16[1024,256]{1,0:T(8,128)(2,1)S(1)}, u32[]{:S(2)}, u32[]{:S(2)}) collective-permute-start(bf16[1024,256]{1,0:T(8,128)(2,1)S(1)} %broadcast_select_fusion.1), channel_id=1, source_target_pairs={{0,16},{2,18},{5,21},{7,23},{8,24},{10,26},{13,29},{15,31},{16,0},... | collective-permute-start | bytes 1572872 | tf_op jit(solution)/shard_map/ppermute | solution.py:31
  60.7 8.6 %collective-permute-start.14 = (bf16[2048,256]{1,0:T(8,128)(2,1)S(1)}, bf16[2048,256]{1,0:T(8,128)(2,1)S(1)}, u32[]{:S(2)}, u32[]{:S(2)}) collective-permute-start(bf16[2048,256]{1,0:T(8,128)(2,1)S(1)} %pad_maximum_fusion.refs_6_), channel_id=1, source_target_pairs={{0,4},{2,6},{5,1},{7,3},{8,12},{10,14},{13,9},{15,11},{16,20},{18,... | collective-permute-start | bytes 3145736 | tf_op jit(solution)/shard_map/ppermute | solution.py:53
  62.2 7.2 %collective-permute-start.15 = (bf16[2048,256]{1,0:T(8,128)(2,1)S(1)}, bf16[2048,256]{1,0:T(8,128)(2,1)S(1)}, u32[]{:S(2)}, u32[]{:S(2)}) collective-permute-start(bf16[2048,256]{1,0:T(8,128)(2,1)S(1)} %pad_maximum_fusion.1.refs_7_), channel_id=1, source_target_pairs={{0,4},{2,6},{5,1},{7,3},{8,12},{10,14},{13,9},{15,11},{16,20},{18,... | collective-permute-start | bytes 3145736 | tf_op jit(solution)/shard_map/ppermute | solution.py:53
  66.4 5.2 %copy-start.2 = (s32[272,2]{0,1:T(2,128)S(1)}, s32[272,2]{0,1:T(2,128)}, u32[]{:S(2)}) copy-start(s32[272,2]{0,1:T(2,128)} %param.9) | copy-start | bytes 6532
  66.4 5.2 %copy-start.4 = (s32[8]{0:T(128)S(1)}, s32[8]{0:T(128)}, u32[]{:S(2)}) copy-start(s32[8]{0:T(128)} %source_list.2) | copy-start | bytes 100
  66.6 3.6 %collective-permute-start.17 = (bf16[2048,256]{1,0:T(8,128)(2,1)S(1)}, bf16[2048,256]{1,0:T(8,128)(2,1)S(1)}, u32[]{:S(2)}, u32[]{:S(2)}) collective-permute-start(bf16[2048,256]{1,0:T(8,128)(2,1)S(1)} %pad_maximum_fusion.3.refs_9_), channel_id=1, source_target_pairs={{0,4},{2,6},{5,1},{7,3},{8,12},{10,14},{13,9},{15,11},{16,20},{18,... | collective-permute-start | bytes 3145736 | tf_op jit(solution)/shard_map/ppermute | solution.py:53
  68.0 3.7 %collective-permute-start.16 = (bf16[2048,256]{1,0:T(8,128)(2,1)S(1)}, bf16[2048,256]{1,0:T(8,128)(2,1)S(1)}, u32[]{:S(2)}, u32[]{:S(2)}) collective-permute-start(bf16[2048,256]{1,0:T(8,128)(2,1)S(1)} %broadcast_select_fusion.refs_8_), channel_id=1, source_target_pairs={{0,4},{2,6},{5,1},{7,3},{8,12},{10,14},{13,9},{15,11},{16,20},{18,... | collective-permute-start | bytes 3145736 | tf_op jit(solution)/shard_map/ppermute | solution.py:53
  71.7 3.4 %copy-start.3 = (s32[264]{0:T(512)S(1)}, s32[264]{0:T(512)}, u32[]{:S(2)}) copy-start(s32[264]{0:T(512)} %source_list.3) | copy-start | bytes 3172
  74.6 26.0 %collective-permute-start.18 = (bf16[8,256,256]{2,1,0:T(8,128)(2,1)S(1)}, bf16[8,256,256]{2,1,0:T(8,128)(2,1)S(1)}, u32[]{:S(2)}, u32[]{:S(2)}) collective-permute-start(bf16[8,256,256]{2,1,0:T(8,128)(2,1)S(1)} %shard_map.77), channel_id=1, source_target_pairs={{0,28},{4,24},{8,20},{12,16},{16,12},{20,8},{24,4},{28,0},{1,29},{... | collective-permute-start | bytes 3145736 | tf_op jit(solution)/shard_map/ppermute | solution.py:275
  100.6 1.6 %copy-start.1 = (f32[1024,256]{1,0:T(8,128)S(1)}, f32[1024,256]{1,0:T(8,128)}, u32[]{:S(2)}) copy-start(f32[1024,256]{1,0:T(8,128)} %param.6) | copy-start | bytes 3145732

commit v3 on v2

--- a/solution.py
+++ b/solution.py
@@ -8,7 +8,7 @@
 
 AXES = ("row", "col")
 RING = 6
-VMEM_LIMIT = 24 * 1024 * 1024
+VMEM_LIMIT = 20 * 1024 * 1024
 
 
 def tied(value, *others):

time: 103 us -> 103 us (level)
  no operation moved by 1% of the time
where the time goes in v3:
time: 103 us; the launch traced here: 102 us
  waiting for transfers between devices  33.3 us (32%)
  starting transfers between devices  32.7 us (32%)
  Pallas kernels  28.8 us (28%)
  other arithmetic  2.69 us (3%)
  matrix products  2.54 us (2%)
  local copies, waits for them, and re-layouts  1.09 us (1%)
    pallas_call x2, Pallas kernels, renew(): pl.pallas_call(functools.partial(renew_kernel, sizes), out_shape=jax.Shap...  27.3 us
    ppermute x2, waiting for transfers between devices, gather_and_spread(): lax.ppermute(half, 'col', [(place, place ^ mask) for place in range(col_c...  12.9 us
    ppermute x4, starting transfers between devices, exchanged(): lax.ppermute(piece, AXES, spread_pairs(bit, known, row_count, col_count))  12.9 us
    ppermute x4, starting transfers between devices, across(): lax.ppermute(value, AXES, spread_pairs(bit, known, row_count, col_count))  9 us
    ppermute x4, waiting for transfers between devices, exchanged(): lax.ppermute(piece, AXES, spread_pairs(bit, known, row_count, col_count))  7.7 us
    ppermute x4, starting transfers between devices, to_other_core(): return lax.ppermute(near, AXES, spread_pairs(0, 1, *sizes))  5.41 us
    ppermute x4, waiting for transfers between devices, across(): lax.ppermute(value, AXES, spread_pairs(bit, known, row_count, col_count))  5.16 us
    ppermute x1, waiting for transfers between devices, gather_and_spread(): onward = lax.ppermute(parts[2], AXES, z_pairs(outer, True))  4.13 us
  transfers between devices with their start and end apart: 19, of which 8 were waited for; matrix products, arithmetic and copies ran while one was open for 2% of the time, Pallas kernels for 24%

profile of v3, /device:TPU:0, one launch (start us, length us, event | category | flops | bytes accessed | tf_op | source)
XLA Modules:
  0.0 102.1 jit_solution(238983518982266910)
XLA Ops:
  0.6 0.0 copy-start
  0.7 1.0 select_reduce_fusion.places
  1.6 0.3 copy-done
  1.9 2.5 %fusion = (bf16[1024,256]{1,0:T(8,128)(2,1)S(1)}, f32[1024,256]{1,0:T(8,128)}) fusion(f32[1024,256]{1,0:T(8,128)S(1)} %copy-done, f32[256,256]{1,0:T(8,128)} %param.7), kind=kOutput, calls=%fused_computation.11 | convolution fusion | flops 402915328 | bytes 2883584 | tf_op jit(solution)/shard_map/dot_general | solution.py:259
  4.4 4.9 %collective-permute-start.6 = (bf16[1024,256]{1,0:T(8,128)(2,1)S(1)}, bf16[1024,256]{1,0:T(8,128)(2,1)S(1)}, u32[]{:S(2)}, u32[]{:S(2)}) collective-permute-start(bf16[1024,256]{1,0:T(8,128)(2,1)S(1)} %get-tuple-element.13.refs_0_), channel_id=1, source_target_pairs={{0,8},{5,13},{10,2},{15,7},{16,24},{21,29},{26,18},{31,23}} | collective-permute-start | bytes 1572872 | tf_op jit(solution)/shard_map/ppermute | solution.py:21
  9.3 0.5 collective-permute-start.1
  9.8 1.0 collective-permute-start
  10.8 5.2 %collective-permute-done.6 = bf16[1024,256]{1,0:T(8,128)(2,1)S(1)} collective-permute-done((bf16[1024,256]{1,0:T(8,128)(2,1)S(1)}, bf16[1024,256]{1,0:T(8,128)(2,1)S(1)}, u32[]{:S(2)}, u32[]{:S(2)}) %collective-permute-start.6) | collective-permute-done | bytes 524320 | tf_op jit(solution)/shard_map/ppermute | solution.py:21
  15.9 0.1 broadcast_select_fusion.3
  16.0 3.4 %collective-permute-start.7 = (bf16[1024,256]{1,0:T(8,128)(2,1)S(1)}, bf16[1024,256]{1,0:T(8,128)(2,1)S(1)}, u32[]{:S(2)}, u32[]{:S(2)}) collective-permute-start(bf16[1024,256]{1,0:T(8,128)(2,1)S(1)} %broadcast_select_fusion.3), channel_id=1, source_target_pairs={{0,16},{2,18},{5,21},{7,23},{8,24},{10,26},{13,29},{15,31},{16,0},... | collective-permute-start | bytes 1572872 | tf_op jit(solution)/shard_map/ppermute | solution.py:31
  19.5 12.9 %collective-permute-done.1.refs_2_ = bf16[1024,256]{1,0:T(8,128)(2,1)S(1)} collective-permute-done((bf16[1024,256]{1,0:T(8,128)(2,1)S(1)}, bf16[1024,256]{1,0:T(8,128)(2,1)S(1)}, u32[]{:S(2)}, u32[]{:S(2)}) %collective-permute-start.1) | collective-permute-done | bytes 524320 | tf_op jit(solution)/shard_map/ppermute | solution.py:65
  32.4 0.7 collective-permute-start.3
  33.1 1.3 %collective-permute-start.2 = (bf16[1024,256]{1,0:T(8,128)(2,1)S(1)}, bf16[1024,256]{1,0:T(8,128)(2,1)S(1)}, u32[]{:S(2)}, u32[]{:S(2)}) collective-permute-start(bf16[1024,256]{1,0:T(8,128)(2,1)S(1)} %collective-permute-done.1.refs_2_), channel_id=1, source_target_pairs={{1,0},{14,15},{17,16},{30,31}} | collective-permute-start | bytes 1572872 | tf_op jit(solution)/shard_map/ppermute | solution.py:72
  34.4 0.0 copy-start.5
  34.4 0.8 copy-done.5
  35.2 3.5 %collective-permute-start.10 = (bf16[1024,256]{1,0:T(8,128)(2,1)S(1)}, bf16[1024,256]{1,0:T(8,128)(2,1)}, u32[]{:S(2)}, u32[]{:S(2)}) collective-permute-start(bf16[1024,256]{1,0:T(8,128)(2,1)S(1)} %collective-permute-done.1.refs_2_), channel_id=1, source_target_pairs={{0,16},{5,21},{10,26},{15,31},{16,0},{21,5},{26,10},{31,15}} | collective-permute-start | bytes 1572872 | tf_op jit(solution)/shard_map/ppermute | solution.py:31
  38.7 1.3 %collective-permute-start.8 = (bf16[1024,256]{1,0:T(8,128)(2,1)S(1)}, bf16[1024,256]{1,0:T(8,128)(2,1)S(1)}, u32[]{:S(2)}, u32[]{:S(2)}) collective-permute-start(bf16[1024,256]{1,0:T(8,128)(2,1)S(1)} %collective-permute-done.refs_1_), channel_id=1, source_target_pairs={{0,8},{5,13},{10,2},{15,7},{16,24},{21,29},{26,18},{31,23}} | collective-permute-start | bytes 1572872 | tf_op jit(solution)/shard_map/ppermute | solution.py:21
  40.0 4.1 %collective-permute-done.2 = bf16[1024,256]{1,0:T(8,128)(2,1)S(1)} collective-permute-done((bf16[1024,256]{1,0:T(8,128)(2,1)S(1)}, bf16[1024,256]{1,0:T(8,128)(2,1)S(1)}, u32[]{:S(2)}, u32[]{:S(2)}) %collective-permute-start.2) | collective-permute-done | bytes 524320 | tf_op jit(solution)/shard_map/ppermute | solution.py:72
  44.1 0.1 broadcast_select_fusion.4.refs_3_
  44.2 1.3 %collective-permute-start.12 = (bf16[1024,256]{1,0:T(8,128)(2,1)S(1)}, bf16[1024,256]{1,0:T(8,128)(2,1)S(1)}, u32[]{:S(2)}, u32[]{:S(2)}) collective-permute-start(bf16[1024,256]{1,0:T(8,128)(2,1)S(1)} %broadcast_select_fusion.4.refs_3_), channel_id=1, source_target_pairs={{0,8},{5,13},{10,2},{15,7},{16,24},{21,29},{26,18},{31,23}} | collective-permute-start | bytes 1572872 | tf_op jit(solution)/shard_map/ppermute | solution.py:21
  45.5 0.7 collective-permute-start.4
  46.2 0.7 collective-permute-start.5
  46.9 1.1 %pad_maximum_fusion.2 = bf16[2048,256]{1,0:T(8,128)(2,1)S(1)} fusion(bf16[1024,256]{1,0:T(8,128)(2,1)} %collective-permute-done.10, bf16[1024,256]{1,0:T(8,128)(2,1)S(1)} %collective-permute-done.1.refs_2_), kind=kLoop, calls=%fused_computation.2 | loop fusion | flops 2097152 | bytes 2097152 | tf_op jit(solution)/shard_map/concatenate | solution.py:74
  48.1 0.0 copy-start.6
  48.1 1.5 %collective-permute-start.11 = (bf16[2048,256]{1,0:T(8,128)(2,1)S(1)}, bf16[2048,256]{1,0:T(8,128)(2,1)S(1)}, u32[]{:S(2)}, u32[]{:S(2)}) collective-permute-start(bf16[2048,256]{1,0:T(8,128)(2,1)S(1)} %pad_maximum_fusion.2), channel_id=1, source_target_pairs={{0,8},{5,13},{10,2},{15,7},{16,24},{21,29},{26,18},{31,23}} | collective-permute-start | bytes 3145736 | tf_op jit(solution)/shard_map/ppermute | solution.py:21
  49.6 0.1 broadcast_select_fusion.2
  49.6 3.5 %collective-permute-start.9 = (bf16[1024,256]{1,0:T(8,128)(2,1)S(1)}, bf16[1024,256]{1,0:T(8,128)(2,1)S(1)}, u32[]{:S(2)}, u32[]{:S(2)}) collective-permute-start(bf16[1024,256]{1,0:T(8,128)(2,1)S(1)} %broadcast_select_fusion.2), channel_id=1, source_target_pairs={{0,16},{2,18},{5,21},{7,23},{8,24},{10,26},{13,29},{15,31},{16,0},... | collective-permute-start | bytes 1572872 | tf_op jit(solution)/shard_map/ppermute | solution.py:31
  53.1 0.1 broadcast_select_fusion.1
  53.2 2.5 %collective-permute-start.13 = (bf16[1024,256]{1,0:T(8,128)(2,1)S(1)}, bf16[1024,256]{1,0:T(8,128)(2,1)S(1)}, u32[]{:S(2)}, u32[]{:S(2)}) collective-permute-start(bf16[1024,256]{1,0:T(8,128)(2,1)S(1)} %broadcast_select_fusion.1), channel_id=1, source_target_pairs={{0,16},{2,18},{5,21},{7,23},{8,24},{10,26},{13,29},{15,31},{16,0},... | collective-permute-start | bytes 1572872 | tf_op jit(solution)/shard_map/ppermute | solution.py:31
  55.7 0.1 pad_maximum_fusion.refs_6_
  55.8 4.9 %collective-permute-done.9 = bf16[1024,256]{1,0:T(8,128)(2,1)S(1)} collective-permute-done((bf16[1024,256]{1,0:T(8,128)(2,1)S(1)}, bf16[1024,256]{1,0:T(8,128)(2,1)S(1)}, u32[]{:S(2)}, u32[]{:S(2)}) %collective-permute-start.9) | collective-permute-done | bytes 524320 | tf_op jit(solution)/shard_map/ppermute | solution.py:31
  60.7 1.3 %collective-permute-start.14 = (bf16[2048,256]{1,0:T(8,128)(2,1)S(1)}, bf16[2048,256]{1,0:T(8,128)(2,1)S(1)}, u32[]{:S(2)}, u32[]{:S(2)}) collective-permute-start(bf16[2048,256]{1,0:T(8,128)(2,1)S(1)} %pad_maximum_fusion.refs_6_), channel_id=1, source_target_pairs={{0,4},{2,6},{5,1},{7,3},{8,12},{10,14},{13,9},{15,11},{16,20},{18,... | collective-permute-start | bytes 3145736 | tf_op jit(solution)/shard_map/ppermute | solution.py:53
  62.1 0.1 pad_maximum_fusion.1.refs_7_
  62.2 1.4 %collective-permute-start.15 = (bf16[2048,256]{1,0:T(8,128)(2,1)S(1)}, bf16[2048,256]{1,0:T(8,128)(2,1)S(1)}, u32[]{:S(2)}, u32[]{:S(2)}) collective-permute-start(bf16[2048,256]{1,0:T(8,128)(2,1)S(1)} %pad_maximum_fusion.1.refs_7_), channel_id=1, source_target_pairs={{0,4},{2,6},{5,1},{7,3},{8,12},{10,14},{13,9},{15,11},{16,20},{18,... | collective-permute-start | bytes 3145736 | tf_op jit(solution)/shard_map/ppermute | solution.py:53
  63.5 2.8 %collective-permute-done.13 = bf16[1024,256]{1,0:T(8,128)(2,1)S(1)} collective-permute-done((bf16[1024,256]{1,0:T(8,128)(2,1)S(1)}, bf16[1024,256]{1,0:T(8,128)(2,1)S(1)}, u32[]{:S(2)}, u32[]{:S(2)}) %collective-permute-start.13) | collective-permute-done | bytes 524320 | tf_op jit(solution)/shard_map/ppermute | solution.py:31
  66.3 0.1 pad_maximum_fusion.3.refs_9_
  66.4 0.0 copy-start.2
  66.4 0.0 copy-start.4
  66.4 0.1 broadcast_select_fusion.refs_8_
  66.6 1.4 %collective-permute-start.17 = (bf16[2048,256]{1,0:T(8,128)(2,1)S(1)}, bf16[2048,256]{1,0:T(8,128)(2,1)S(1)}, u32[]{:S(2)}, u32[]{:S(2)}) collective-permute-start(bf16[2048,256]{1,0:T(8,128)(2,1)S(1)} %pad_maximum_fusion.3.refs_9_), channel_id=1, source_target_pairs={{0,4},{2,6},{5,1},{7,3},{8,12},{10,14},{13,9},{15,11},{16,20},{18,... | collective-permute-start | bytes 3145736 | tf_op jit(solution)/shard_map/ppermute | solution.py:53
  68.0 1.4 %collective-permute-start.16 = (bf16[2048,256]{1,0:T(8,128)(2,1)S(1)}, bf16[2048,256]{1,0:T(8,128)(2,1)S(1)}, u32[]{:S(2)}, u32[]{:S(2)}) collective-permute-start(bf16[2048,256]{1,0:T(8,128)(2,1)S(1)} %broadcast_select_fusion.refs_8_), channel_id=1, source_target_pairs={{0,4},{2,6},{5,1},{7,3},{8,12},{10,14},{13,9},{15,11},{16,20},{18,... | collective-permute-start | bytes 3145736 | tf_op jit(solution)/shard_map/ppermute | solution.py:53
  69.3 0.8 collective-permute-done.17.refs_13_
  70.2 1.5 %collective-permute-done.16.refs_12_ = bf16[2048,256]{1,0:T(8,128)(2,1)S(1)} collective-permute-done((bf16[2048,256]{1,0:T(8,128)(2,1)S(1)}, bf16[2048,256]{1,0:T(8,128)(2,1)S(1)}, u32[]{:S(2)}, u32[]{:S(2)}) %collective-permute-start.16) | collective-permute-done | bytes 1048608 | tf_op jit(solution)/shard_map/ppermute | solution.py:53
  71.7 2.9 %shard_map.77 = bf16[8,256,256]{2,1,0:T(8,128)(2,1)S(1)} custom-call(s32[8]{0:T(128)S(1)} %copy-done.4, s32[2,272]{1,0:T(2,128)S(1)} %bitcast.3, bf16[1024,256]{1,0:T(8,128)(2,1)S(1)} %get-tuple-element.13.refs_0_, bf16[1024,256]{1,0:T(8,128)(2,1)S(1)} %collective-permute-done.refs_1_, bf16[1024,256]{1,0:T(8,128)(2,1)S(1)} %collective-permute-done.1.refs_2_, ...), custom_call_target="tpu_custom_call" | custom-call | flops 268435456 | bytes 8388608 | tf_op jit(solution)/shard_map/pallas_call | solution.py:194
  74.6 0.5 collective-permute-start.18
  75.1 24.3 %shard_map.78.held = bf16[264,256,256]{2,1,0:T(8,128)(2,1)} custom-call(s32[264]{0:T(512)S(1)} %copy-done.3, s32[2,272]{1,0:T(2,128)S(1)} %bitcast.4, bf16[1024,256]{1,0:T(8,128)(2,1)S(1)} %get-tuple-element.13.refs_0_, bf16[1024,256]{1,0:T(8,128)(2,1)S(1)} %collective-permute-done.refs_1_, bf16[1024,256]{1,0:T(8,128)(2,1)S(1)} %collective-permute-done.1.refs_2_, ...), custom_call_target="tpu_custom_call" | custom-call | flops 8858370048 | bytes 75497472 | tf_op jit(solution)/shard_map/pallas_call | solution.py:194
  99.5 1.1 %collective-permute-done.18.incoming = bf16[8,256,256]{2,1,0:T(8,128)(2,1)S(1)} collective-permute-done((bf16[8,256,256]{2,1,0:T(8,128)(2,1)S(1)}, bf16[8,256,256]{2,1,0:T(8,128)(2,1)S(1)}, u32[]{:S(2)}, u32[]{:S(2)}) %collective-permute-start.18) | collective-permute-done | bytes 1048608 | tf_op jit(solution)/shard_map/ppermute | solution.py:275
  100.6 1.6 %shard_map.79 = bf16[264,256,256]{2,1,0:T(8,128)(2,1)} custom-call(s32[8]{0:T(128)S(1)} %select_reduce_fusion.places, bf16[8,256,256]{2,1,0:T(8,128)(2,1)S(1)} %collective-permute-done.18.incoming, bf16[264,256,256]{2,1,0:T(8,128)(2,1)} %shard_map.78.held), custom_call_target="tpu_custom_call", output_to_operand_aliasing={{}: (2, {})} | custom-call | tf_op jit(solution)/shard_map/pallas_call | solution.py:236
  (19 shorter events, 0.0 us)
Async XLA Ops:
  0.6 1.2 %copy-start = (f32[1024,256]{1,0:T(8,128)S(1)}, f32[1024,256]{1,0:T(8,128)}, u32[]{:S(2)}) copy-start(f32[1024,256]{1,0:T(8,128)} %param.6) | copy-start | bytes 3145732
  4.4 11.5 %collective-permute-start.6 = (bf16[1024,256]{1,0:T(8,128)(2,1)S(1)}, bf16[1024,256]{1,0:T(8,128)(2,1)S(1)}, u32[]{:S(2)}, u32[]{:S(2)}) collective-permute-start(bf16[1024,256]{1,0:T(8,128)(2,1)S(1)} %get-tuple-element.13.refs_0_), channel_id=1, source_target_pairs={{0,8},{5,13},{10,2},{15,7},{16,24},{21,29},{26,18},{31,23}} | collective-permute-start | bytes 1572872 | tf_op jit(solution)/shard_map/ppermute | solution.py:21
  9.3 23.1 %collective-permute-start.1 = (bf16[1024,256]{1,0:T(8,128)(2,1)S(1)}, bf16[1024,256]{1,0:T(8,128)(2,1)S(1)}, u32[]{:S(2)}, u32[]{:S(2)}) collective-permute-start(bf16[1024,256]{1,0:T(8,128)(2,1)S(1)} %get-tuple-element.13.refs_0_), channel_id=1, source_target_pairs={{0,2},{1,3},{2,0},{3,1},{4,6},{5,7},{6,4},{7,5},{8,10},{9,11},{10,... | collective-permute-start | bytes 1572872 | tf_op jit(solution)/shard_map/ppermute | solution.py:65
  9.8 24.6 %collective-permute-start = (bf16[1024,256]{1,0:T(8,128)(2,1)S(1)}, bf16[1024,256]{1,0:T(8,128)(2,1)S(1)}, u32[]{:S(2)}, u32[]{:S(2)}) collective-permute-start(bf16[1024,256]{1,0:T(8,128)(2,1)S(1)} %get-tuple-element.13.refs_0_), channel_id=1, source_target_pairs={{0,1},{1,0},{2,3},{3,2},{4,5},{5,4},{6,7},{7,6},{8,9},{9,8},{10,11... | collective-permute-start | bytes 1572872 | tf_op jit(solution)/shard_map/ppermute | solution.py:65
  16.0 18.4 %collective-permute-start.7 = (bf16[1024,256]{1,0:T(8,128)(2,1)S(1)}, bf16[1024,256]{1,0:T(8,128)(2,1)S(1)}, u32[]{:S(2)}, u32[]{:S(2)}) collective-permute-start(bf16[1024,256]{1,0:T(8,128)(2,1)S(1)} %broadcast_select_fusion.3), channel_id=1, source_target_pairs={{0,16},{2,18},{5,21},{7,23},{8,24},{10,26},{13,29},{15,31},{16,0},... | collective-permute-start | bytes 1572872 | tf_op jit(solution)/shard_map/ppermute | solution.py:31
  32.4 7.6 %collective-permute-start.3 = (bf16[1024,256]{1,0:T(8,128)(2,1)S(1)}, bf16[1024,256]{1,0:T(8,128)(2,1)S(1)}, u32[]{:S(2)}, u32[]{:S(2)}) collective-permute-start(bf16[1024,256]{1,0:T(8,128)(2,1)S(1)} %get-tuple-element.13.refs_0_), channel_id=1, source_target_pairs={{6,5},{9,10},{22,21},{25,26}} | collective-permute-start | bytes 1572872 | tf_op jit(solution)/shard_map/ppermute | solution.py:71
  33.1 11.1 %collective-permute-start.2 = (bf16[1024,256]{1,0:T(8,128)(2,1)S(1)}, bf16[1024,256]{1,0:T(8,128)(2,1)S(1)}, u32[]{:S(2)}, u32[]{:S(2)}) collective-permute-start(bf16[1024,256]{1,0:T(8,128)(2,1)S(1)} %collective-permute-done.1.refs_2_), channel_id=1, source_target_pairs={{1,0},{14,15},{17,16},{30,31}} | collective-permute-start | bytes 1572872 | tf_op jit(solution)/shard_map/ppermute | solution.py:72
  34.4 0.8 copy-start.5
  35.2 11.8 %collective-permute-start.10 = (bf16[1024,256]{1,0:T(8,128)(2,1)S(1)}, bf16[1024,256]{1,0:T(8,128)(2,1)}, u32[]{:S(2)}, u32[]{:S(2)}) collective-permute-start(bf16[1024,256]{1,0:T(8,128)(2,1)S(1)} %collective-permute-done.1.refs_2_), channel_id=1, source_target_pairs={{0,16},{5,21},{10,26},{15,31},{16,0},{21,5},{26,10},{31,15}} | collective-permute-start | bytes 1572872 | tf_op jit(solution)/shard_map/ppermute | solution.py:31
  38.7 10.9 %collective-permute-start.8 = (bf16[1024,256]{1,0:T(8,128)(2,1)S(1)}, bf16[1024,256]{1,0:T(8,128)(2,1)S(1)}, u32[]{:S(2)}, u32[]{:S(2)}) collective-permute-start(bf16[1024,256]{1,0:T(8,128)(2,1)S(1)} %collective-permute-done.refs_1_), channel_id=1, source_target_pairs={{0,8},{5,13},{10,2},{15,7},{16,24},{21,29},{26,18},{31,23}} | collective-permute-start | bytes 1572872 | tf_op jit(solution)/shard_map/ppermute | solution.py:21
  44.2 8.9 %collective-permute-start.12 = (bf16[1024,256]{1,0:T(8,128)(2,1)S(1)}, bf16[1024,256]{1,0:T(8,128)(2,1)S(1)}, u32[]{:S(2)}, u32[]{:S(2)}) collective-permute-start(bf16[1024,256]{1,0:T(8,128)(2,1)S(1)} %broadcast_select_fusion.4.refs_3_), channel_id=1, source_target_pairs={{0,8},{5,13},{10,2},{15,7},{16,24},{21,29},{26,18},{31,23}} | collective-permute-start | bytes 1572872 | tf_op jit(solution)/shard_map/ppermute | solution.py:21
  45.5 16.6 %collective-permute-start.4 = (bf16[1024,256]{1,0:T(8,128)(2,1)S(1)}, bf16[1024,256]{1,0:T(8,128)(2,1)S(1)}, u32[]{:S(2)}, u32[]{:S(2)}) collective-permute-start(bf16[1024,256]{1,0:T(8,128)(2,1)S(1)} %collective-permute-done.1.refs_2_), channel_id=1, source_target_pairs={{2,3},{5,4},{6,7},{9,8},{10,11},{13,12},{18,19},{21,20},{22,23},{2... | collective-permute-start | bytes 1572872 | tf_op jit(solution)/shard_map/ppermute | solution.py:77
  46.2 15.9 %collective-permute-start.5 = (bf16[1024,256]{1,0:T(8,128)(2,1)S(1)}, bf16[1024,256]{1,0:T(8,128)(2,1)S(1)}, u32[]{:S(2)}, u32[]{:S(2)}) collective-permute-start(bf16[1024,256]{1,0:T(8,128)(2,1)S(1)} %get-tuple-element.13.refs_0_), channel_id=1, source_target_pairs={{1,2},{2,1},{5,6},{10,9},{13,14},{14,13},{17,18},{18,17},{21,22},{... | collective-permute-start | bytes 1572872 | tf_op jit(solution)/shard_map/ppermute | solution.py:76
  48.1 7.7 %copy-start.6 = (bf16[1024,256]{1,0:T(8,128)(2,1)S(1)}, bf16[1024,256]{1,0:T(8,128)(2,1)}, u32[]{:S(2)}) copy-start(bf16[1024,256]{1,0:T(8,128)(2,1)} %copy-done.5) | copy-start | bytes 1572868
  48.1 18.4 %collective-permute-start.11 = (bf16[2048,256]{1,0:T(8,128)(2,1)S(1)}, bf16[2048,256]{1,0:T(8,128)(2,1)S(1)}, u32[]{:S(2)}, u32[]{:S(2)}) collective-permute-start(bf16[2048,256]{1,0:T(8,128)(2,1)S(1)} %pad_maximum_fusion.2), channel_id=1, source_target_pairs={{0,8},{5,13},{10,2},{15,7},{16,24},{21,29},{26,18},{31,23}} | collective-permute-start | bytes 3145736 | tf_op jit(solution)/shard_map/ppermute | solution.py:21
  49.6 11.1 %collective-permute-start.9 = (bf16[1024,256]{1,0:T(8,128)(2,1)S(1)}, bf16[1024,256]{1,0:T(8,128)(2,1)S(1)}, u32[]{:S(2)}, u32[]{:S(2)}) collective-permute-start(bf16[1024,256]{1,0:T(8,128)(2,1)S(1)} %broadcast_select_fusion.2), channel_id=1, source_target_pairs={{0,16},{2,18},{5,21},{7,23},{8,24},{10,26},{13,29},{15,31},{16,0},... | collective-permute-start | bytes 1572872 | tf_op jit(solution)/shard_map/ppermute | solution.py:31
  53.2 13.1 %collective-permute-start.13 = (bf16[1024,256]{1,0:T(8,128)(2,1)S(1)}, bf16[1024,256]{1,0:T(8,128)(2,1)S(1)}, u32[]{:S(2)}, u32[]{:S(2)}) collective-permute-start(bf16[1024,256]{1,0:T(8,128)(2,1)S(1)} %broadcast_select_fusion.1), channel_id=1, source_target_pairs={{0,16},{2,18},{5,21},{7,23},{8,24},{10,26},{13,29},{15,31},{16,0},... | collective-permute-start | bytes 1572872 | tf_op jit(solution)/shard_map/ppermute | solution.py:31
  60.7 8.6 %collective-permute-start.14 = (bf16[2048,256]{1,0:T(8,128)(2,1)S(1)}, bf16[2048,256]{1,0:T(8,128)(2,1)S(1)}, u32[]{:S(2)}, u32[]{:S(2)}) collective-permute-start(bf16[2048,256]{1,0:T(8,128)(2,1)S(1)} %pad_maximum_fusion.refs_6_), channel_id=1, source_target_pairs={{0,4},{2,6},{5,1},{7,3},{8,12},{10,14},{13,9},{15,11},{16,20},{18,... | collective-permute-start | bytes 3145736 | tf_op jit(solution)/shard_map/ppermute | solution.py:53
  62.2 7.2 %collective-permute-start.15 = (bf16[2048,256]{1,0:T(8,128)(2,1)S(1)}, bf16[2048,256]{1,0:T(8,128)(2,1)S(1)}, u32[]{:S(2)}, u32[]{:S(2)}) collective-permute-start(bf16[2048,256]{1,0:T(8,128)(2,1)S(1)} %pad_maximum_fusion.1.refs_7_), channel_id=1, source_target_pairs={{0,4},{2,6},{5,1},{7,3},{8,12},{10,14},{13,9},{15,11},{16,20},{18,... | collective-permute-start | bytes 3145736 | tf_op jit(solution)/shard_map/ppermute | solution.py:53
  66.4 5.2 %copy-start.2 = (s32[272,2]{0,1:T(2,128)S(1)}, s32[272,2]{0,1:T(2,128)}, u32[]{:S(2)}) copy-start(s32[272,2]{0,1:T(2,128)} %param.9) | copy-start | bytes 6532
  66.4 5.2 %copy-start.4 = (s32[8]{0:T(128)S(1)}, s32[8]{0:T(128)}, u32[]{:S(2)}) copy-start(s32[8]{0:T(128)} %source_list.2) | copy-start | bytes 100
  66.6 3.6 %collective-permute-start.17 = (bf16[2048,256]{1,0:T(8,128)(2,1)S(1)}, bf16[2048,256]{1,0:T(8,128)(2,1)S(1)}, u32[]{:S(2)}, u32[]{:S(2)}) collective-permute-start(bf16[2048,256]{1,0:T(8,128)(2,1)S(1)} %pad_maximum_fusion.3.refs_9_), channel_id=1, source_target_pairs={{0,4},{2,6},{5,1},{7,3},{8,12},{10,14},{13,9},{15,11},{16,20},{18,... | collective-permute-start | bytes 3145736 | tf_op jit(solution)/shard_map/ppermute | solution.py:53
  68.0 3.7 %collective-permute-start.16 = (bf16[2048,256]{1,0:T(8,128)(2,1)S(1)}, bf16[2048,256]{1,0:T(8,128)(2,1)S(1)}, u32[]{:S(2)}, u32[]{:S(2)}) collective-permute-start(bf16[2048,256]{1,0:T(8,128)(2,1)S(1)} %broadcast_select_fusion.refs_8_), channel_id=1, source_target_pairs={{0,4},{2,6},{5,1},{7,3},{8,12},{10,14},{13,9},{15,11},{16,20},{18,... | collective-permute-start | bytes 3145736 | tf_op jit(solution)/shard_map/ppermute | solution.py:53
  71.7 3.4 %copy-start.3 = (s32[264]{0:T(512)S(1)}, s32[264]{0:T(512)}, u32[]{:S(2)}) copy-start(s32[264]{0:T(512)} %source_list.3) | copy-start | bytes 3172
  74.6 26.0 %collective-permute-start.18 = (bf16[8,256,256]{2,1,0:T(8,128)(2,1)S(1)}, bf16[8,256,256]{2,1,0:T(8,128)(2,1)S(1)}, u32[]{:S(2)}, u32[]{:S(2)}) collective-permute-start(bf16[8,256,256]{2,1,0:T(8,128)(2,1)S(1)} %shard_map.77), channel_id=1, source_target_pairs={{0,28},{4,24},{8,20},{12,16},{16,12},{20,8},{24,4},{28,0},{1,29},{... | collective-permute-start | bytes 3145736 | tf_op jit(solution)/shard_map/ppermute | solution.py:275
  100.6 1.6 %copy-start.1 = (f32[1024,256]{1,0:T(8,128)S(1)}, f32[1024,256]{1,0:T(8,128)}, u32[]{:S(2)}) copy-start(f32[1024,256]{1,0:T(8,128)} %param.6) | copy-start | bytes 3145732
